TPU v7x, 256 devices: a whole 4x4x8 slice. The times are simulated.
256 devices in a mesh: outer: 8 (over y, z_hi), inner: 32 (over z_lo, x, core).
Axes of the slice: x: 4, y: 4, z: 8 (z_hi: 2, z_lo: 4; z = z_hi * 4 + z_lo), core: 2. Of those that a mesh axis runs over, the one named last changes fastest.
Arguments:
- query: bfloat16 [32768, 24, 128], P(('outer', 'inner')), may hold values from -6 to 6
- key: bfloat16 [32768, 4, 128], P(('outer', 'inner')), may hold values from -6 to 6
- value: bfloat16 [32768, 4, 128], P(('outer', 'inner')), may hold values from -0.625 to 0.625
- output: bfloat16 [32768, 24, 128], P(('outer', 'inner')), may hold values from -0.625 to 0.625
- grad_output: bfloat16 [32768, 24, 128], P(('outer', 'inner')), may hold values from -6 to 6
- lse: float32 [24, 32768], P(None, ('outer', 'inner')), may hold values from 2 to 5
- doc_starts: int32 [24], replicated, may hold values from 0 to 31232, as said below
Outputs:
- grad_query: bfloat16 [32768, 24, 128], P(('outer', 'inner'))
- grad_key: bfloat16 [32768, 4, 128], P(('outer', 'inner'))
- grad_value: bfloat16 [32768, 4, 128], P(('outer', 'inner'))
Inputs may be any that keep to these rules, and one draw needn't show every extreme that they name: `doc_starts`: strictly increasing, the first entry 0. Window w holds positions w * 4096 to (w + 1) * 4096 - 1. Entries 3w + 1 and 3w + 2 lie inside window w; for w >= 1, entry 3w lies within the last 1536 positions of window w - 1, and entry 3w + 1 is at most w * 4096 + 4096 // 4. No document is longer than 2560 tokens.
All inputs are finite; a program needn't handle non-finite values.
Results may differ from a plain program's by a relative error of at most 0.02.
Values may be sent and summed in bfloat16 or wider, within the bound.
A program may use at most 128 MiB of HBM per device.

v0:
```python
import math

import jax
import jax.numpy as jnp
from jax import lax
from jax.sharding import PartitionSpec as P


def from_behind(block, axis, distance):
    devices = range(lax.axis_size(axis))
    route = [(i - distance, i) for i in devices if i - distance in devices]
    return lax.ppermute(block, axis, route)


def doc_number(positions, doc_starts):
    return jnp.sum((doc_starts[None, :] <= positions[:, None]).astype(jnp.int32), axis=1) - 1


def block_grads(
    query_rows,
    grad_rows,
    lse_rows,
    delta_rows,
    query_pos,
    query_doc,
    key_rows,
    value_rows,
    key_pos,
    key_doc,
    score_scale,
):
    scores = (
        jnp.einsum("qhgd,khd->hgqk", query_rows, key_rows, preferred_element_type=jnp.float32)
        * score_scale
    )
    allowed = (key_pos[None, :] <= query_pos[:, None]) & (key_doc[None, :] == query_doc[:, None])
    weights = jnp.where(allowed, jnp.exp(scores - lse_rows[..., None]), 0.0)
    grad_weights = jnp.einsum(
        "qhgd,khd->hgqk", grad_rows, value_rows, preferred_element_type=jnp.float32
    )
    grad_scores = (weights * (grad_weights - delta_rows[..., None])).astype(jnp.bfloat16)
    weights_low = weights.astype(jnp.bfloat16)
    query_part = jnp.einsum(
        "hgqk,khd->qhgd", grad_scores, key_rows, preferred_element_type=jnp.float32
    )
    key_part = jnp.einsum(
        "hgqk,qhgd->khd", grad_scores, query_rows, preferred_element_type=jnp.float32
    )
    value_part = jnp.einsum(
        "hgqk,qhgd->khd", weights_low, grad_rows, preferred_element_type=jnp.float32
    )
    return (query_part, key_part, value_part)


def gated_grads(active, query_side, key_side, score_scale):
    query_rows, grad_rows, lse_rows, delta_rows, query_pos, query_doc = query_side
    key_rows, value_rows, key_pos, key_doc = key_side

    def compute():
        return block_grads(
            query_rows,
            grad_rows,
            lse_rows,
            delta_rows,
            query_pos,
            query_doc,
            key_rows,
            value_rows,
            key_pos,
            key_doc,
            score_scale,
        )

    def skipped():
        return (
            jnp.zeros(query_rows.shape, jnp.float32),
            jnp.zeros(key_rows.shape, jnp.float32),
            jnp.zeros(key_rows.shape, jnp.float32),
        )

    return lax.cond(active, compute, skipped)


def on_device(query, key, value, output, grad_output, lse, doc_starts):
    tok_rows, query_heads, head_width = query.shape
    key_heads = key.shape[1]
    group_size = query_heads // key_heads
    part_rows = tok_rows // 2
    inner_count = lax.axis_size("inner")
    half_window = part_rows * inner_count
    window_rows = 2 * half_window
    block_rows = min(512, half_window)
    block_total = half_window // block_rows
    score_scale = 1.0 / math.sqrt(head_width)
    window = lax.axis_index("outer")
    device = lax.axis_index("inner")
    window_base = window * window_rows
    offsets = jnp.arange(part_rows, dtype=jnp.int32)
    first_pos = window_base + device * part_rows + offsets
    second_pos = window_base + (2 * inner_count - 1 - device) * part_rows + offsets
    grouped = query.reshape(tok_rows, key_heads, group_size, head_width)
    grad_grouped = grad_output.reshape(tok_rows, key_heads, group_size, head_width)
    lse_grouped = lse.reshape(key_heads, group_size, tok_rows)
    delta = jnp.einsum(
        "qhd,qhd->hq", grad_output, output, preferred_element_type=jnp.float32
    ).reshape(key_heads, group_size, tok_rows)
    first_side = (
        grouped[:part_rows],
        grad_grouped[:part_rows],
        lse_grouped[:, :, :part_rows],
        delta[:, :, :part_rows],
        first_pos,
        doc_number(first_pos, doc_starts),
    )
    second_side = (
        grouped[part_rows:],
        grad_grouped[part_rows:],
        lse_grouped[:, :, part_rows:],
        delta[:, :, part_rows:],
        second_pos,
        doc_number(second_pos, doc_starts),
    )
    shifted = from_behind((key[part_rows:], value[part_rows:]), "outer", 1)
    window_keys, window_values = (
        lax.all_gather(
            key.reshape(2, part_rows, key_heads, head_width), "inner", axis=1, tiled=True
        ),
        lax.all_gather(
            value.reshape(2, part_rows, key_heads, head_width), "inner", axis=1, tiled=True
        ),
    )
    prior_keys, prior_values = (
        lax.all_gather(shifted[0], "inner", axis=0, tiled=True),
        lax.all_gather(shifted[1], "inner", axis=0, tiled=True),
    )
    rows_half = jnp.arange(half_window, dtype=jnp.int32)
    lower_pos = window_base + rows_half
    upper_pos = (
        window_base + window_rows - part_rows * (rows_half // part_rows + 1) + rows_half % part_rows
    )
    prior_pos = upper_pos - window_rows
    lower_doc = doc_number(lower_pos, doc_starts)
    upper_doc = doc_number(upper_pos, doc_starts)
    prior_doc = doc_number(prior_pos, doc_starts)
    first_high = ((device + 1) * part_rows - 1) // block_rows + 1
    upper_low = device * part_rows // block_rows
    first_low = 0
    second_low = 0

    def step(block_index, totals):
        first_grad, second_grad, own_keys, own_values, back_keys, back_values = totals
        row_start = block_index * block_rows

        def key_side(key_source, value_source, pos_source, doc_source):
            return (
                lax.dynamic_slice_in_dim(key_source, row_start, block_rows, 0),
                lax.dynamic_slice_in_dim(value_source, row_start, block_rows, 0),
                lax.dynamic_slice_in_dim(pos_source, row_start, block_rows, 0),
                lax.dynamic_slice_in_dim(doc_source, row_start, block_rows, 0),
            )

        lower_side = key_side(window_keys[0], window_values[0], lower_pos, lower_doc)
        upper_side = key_side(window_keys[1], window_values[1], upper_pos, upper_doc)
        prior_side = key_side(prior_keys, prior_values, prior_pos, prior_doc)
        lower_first = gated_grads(
            (block_index >= first_low) & (block_index < first_high),
            first_side,
            lower_side,
            score_scale,
        )
        lower_second = gated_grads(block_index >= second_low, second_side, lower_side, score_scale)
        upper_second = gated_grads(
            (block_index >= upper_low) & (block_index < block_total),
            second_side,
            upper_side,
            score_scale,
        )
        prior_first = gated_grads(block_index < block_total, first_side, prior_side, score_scale)
        first_grad = first_grad + lower_first[0] + prior_first[0]
        second_grad = second_grad + lower_second[0] + upper_second[0]
        new_keys = jnp.stack(
            [(lower_first[1] + lower_second[1]) * score_scale, upper_second[1] * score_scale]
        ).astype(jnp.bfloat16)
        new_values = jnp.stack([lower_first[2] + lower_second[2], upper_second[2]]).astype(
            jnp.bfloat16
        )
        own_keys = lax.dynamic_update_slice(own_keys, new_keys, (0, row_start, 0, 0))
        own_values = lax.dynamic_update_slice(own_values, new_values, (0, row_start, 0, 0))
        back_keys = lax.dynamic_update_slice_in_dim(
            back_keys, (prior_first[1] * score_scale).astype(jnp.bfloat16), row_start, 0
        )
        back_values = lax.dynamic_update_slice_in_dim(
            back_values, prior_first[2].astype(jnp.bfloat16), row_start, 0
        )
        return (first_grad, second_grad, own_keys, own_values, back_keys, back_values)

    query_zeros = jnp.zeros((part_rows, key_heads, group_size, head_width), jnp.float32)
    own_zeros = jnp.zeros((2, half_window, key_heads, head_width), jnp.bfloat16)
    back_zeros = jnp.zeros((half_window, key_heads, head_width), jnp.bfloat16)
    first_grad, second_grad, own_keys, own_values, back_keys, back_values = lax.fori_loop(
        0,
        block_total,
        step,
        (query_zeros, query_zeros, own_zeros, own_zeros, back_zeros, back_zeros),
    )
    grad_query = (
        (jnp.concatenate([first_grad, second_grad], axis=0) * score_scale)
        .astype(jnp.bfloat16)
        .reshape(tok_rows, query_heads, head_width)
    )
    summed_keys, summed_values = (
        lax.psum_scatter(own_keys, "inner", scatter_dimension=1, tiled=True).astype(jnp.float32),
        lax.psum_scatter(own_values, "inner", scatter_dimension=1, tiled=True).astype(jnp.float32),
    )
    prior_sum_keys, prior_sum_values = (
        lax.psum_scatter(back_keys, "inner", scatter_dimension=0, tiled=True).astype(jnp.float32),
        lax.psum_scatter(back_values, "inner", scatter_dimension=0, tiled=True).astype(jnp.float32),
    )
    returned_keys, returned_values = (
        from_behind(prior_sum_keys.astype(jnp.bfloat16), "outer", -1).astype(prior_sum_keys.dtype),
        from_behind(prior_sum_values.astype(jnp.bfloat16), "outer", -1).astype(
            prior_sum_values.dtype
        ),
    )
    grad_key = (
        jnp.stack([summed_keys[0], summed_keys[1] + returned_keys])
        .reshape(tok_rows, key_heads, head_width)
        .astype(jnp.bfloat16)
    )
    grad_value = (
        jnp.stack([summed_values[0], summed_values[1] + returned_values])
        .reshape(tok_rows, key_heads, head_width)
        .astype(jnp.bfloat16)
    )
    return (grad_query, grad_key, grad_value)


def solution(mesh):
    return jax.shard_map(
        on_device,
        mesh=mesh,
        in_specs=(
            P(("outer", "inner"), None, None),
            P(("outer", "inner"), None, None),
            P(("outer", "inner"), None, None),
            P(("outer", "inner"), None, None),
            P(("outer", "inner"), None, None),
            P(None, ("outer", "inner")),
            P(),
        ),
        out_specs=(
            P(("outer", "inner"), None, None),
            P(("outer", "inner"), None, None),
            P(("outer", "inner"), None, None),
        ),
        check_vma=False,
    )
```

profile of v0, /device:TPU:16, one launch (start us, length us, event | category | flops | bytes accessed | tf_op | source)
XLA Modules:
  0.0 992.8 jit_solution(2771254006824869504)
XLA Ops:
  11.5 9.1 collective-permute-start
  20.6 3.0 collective-permute-done
  25.2 8.3 collective-permute-start.1
  33.4 4.0 collective-permute-done.1
  44.0 33.4 %all-gather.5.cloned.1.call-done = bf16[2,2048,4,128]{3,1,0,2:T(8,128)(2,1)} async-done(((bf16[2,64,4,128]{3,1,0,2:T(8,128)(2,1)}), bf16[2,2048,4,128]{3,1,0,2:T(8,128)(2,1)}) %all-gather.5.cloned.1.call-update) | async-done | bytes 4194320 | tf_op jit(solution)/shard_map/all_gather | solution.py:125
  77.5 4.4 copy.41
  81.9 59.3 %all-gather.7.cloned.1.call-done = bf16[2,2048,4,128]{3,1,0,2:T(8,128)(2,1)} async-done(((bf16[2,64,4,128]{3,1,0,2:T(8,128)(2,1)}), bf16[2,2048,4,128]{3,1,0,2:T(8,128)(2,1)}) %all-gather.7.cloned.1.call-update) | async-done | bytes 4194320 | tf_op jit(solution)/shard_map/all_gather | solution.py:128
  141.2 4.5 copy.42
  145.7 56.4 %all-gather.9.cloned.1.call-done = bf16[2048,4,128]{2,0,1:T(8,128)(2,1)} async-done(((bf16[64,4,128]{2,0,1:T(8,128)(2,1)}), bf16[2048,4,128]{2,0,1:T(8,128)(2,1)}) %all-gather.9.cloned.1.call-update) | async-done | bytes 2097168 | tf_op jit(solution)/shard_map/all_gather | solution.py:133
  202.1 60.9 %all-gather.11.cloned.1.call-done = bf16[2048,4,128]{2,0,1:T(8,128)(2,1)} async-done(((bf16[64,4,128]{2,0,1:T(8,128)(2,1)}), bf16[2048,4,128]{2,0,1:T(8,128)(2,1)}) %all-gather.11.cloned.1.call-update) | async-done | bytes 2097168 | tf_op jit(solution)/shard_map/all_gather | solution.py:134
  266.2 2.5 broadcast_in_dim.56.clone
  268.7 2.6 broadcast_in_dim.56
  271.3 119.7 %while.24 = (s32[]{:T(128)}, f32[64,4,6,128]{3,0,2,1:T(8,128)}, f32[64,4,6,128]{3,0,2,1:T(8,128)}, bf16[2,2048,4,128]{3,1,2,0:T(8,128)(2,1)}, bf16[2,2048,4,128]...) while((s32[]{:T(128)}, f32[64,4,6,128]{3,0,2,1:T(8,128)}, ...), condition=%wide.region_12.13_spmd.clone, body=%wide.region_5.12_spmd.clone.sunk | while | flops 4066657792 | bytes 198538512 | solution.py:200
  276.5 4.9 conditional.10
  282.6 4.8 conditional.9
  288.4 4.8 conditional.11
  296.5 2.2 fusion.201
  309.9 4.9 conditional.10
  317.2 4.8 conditional.11
  325.3 2.2 fusion.201
  338.7 4.9 conditional.10
  346.0 4.9 conditional.11
  354.1 2.2 fusion.201
  367.4 4.9 conditional.10
  374.7 4.8 conditional.11
  382.8 2.2 fusion.201
  393.1 144.5 %reduce-scatter.7.cloned.1.call-done = bf16[64,4,128]{2,0,1:T(8,128)(2,1)} async-done(((bf16[2048,4,128]{2,0,1:T(8,128)(2,1)}), bf16[64,4,128]{2,0,1:T(8,128)(2,1)}) %reduce-scatter.7.cloned.1.call-update) | async-done | bytes 65552 | tf_op jit(solution)/shard_map/reduce_scatter | solution.py:216
  537.6 5.1 collective-permute-start.2
  544.4 139.8 %reduce-scatter.11.cloned.1.call-done = bf16[64,4,128]{2,0,1:T(8,128)(2,1)} async-done(((bf16[2048,4,128]{2,0,1:T(8,128)(2,1)}), bf16[64,4,128]{2,0,1:T(8,128)(2,1)}) %reduce-scatter.11.cloned.1.call-update) | async-done | bytes 65552 | tf_op jit(solution)/shard_map/reduce_scatter | solution.py:217
  684.2 5.1 collective-permute-start.3
  689.2 144.5 %reduce-scatter.5.cloned.1.call-done = bf16[2,64,4,128]{3,1,2,0:T(8,128)(2,1)} async-done(((bf16[2,2048,4,128]{3,1,2,0:T(8,128)(2,1)}), bf16[2,64,4,128]{3,1,2,0:T(8,128)(2,1)}) %reduce-scatter.5.cloned.1.call-update) | async-done | bytes 131088 | tf_op jit(solution)/shard_map/reduce_scatter | solution.py:212
  836.3 147.2 %reduce-scatter.9.cloned.1.call-done = bf16[2,64,4,128]{3,1,2,0:T(8,128)(2,1)} async-done(((bf16[2,2048,4,128]{3,1,2,0:T(8,128)(2,1)}), bf16[2,64,4,128]{3,1,2,0:T(8,128)(2,1)}) %reduce-scatter.9.cloned.1.call-update) | async-done | bytes 131088 | tf_op jit(solution)/shard_map/reduce_scatter | solution.py:213
  (481 shorter events, 133.9 us)
Async XLA Ops:
  7.2 34.0 %copy-start.18 = (bf16[128,24,128]{2,1,0:T(8,128)(2,1)S(1)}, bf16[128,24,128]{2,1,0:T(8,128)(2,1)}, u32[]{:S(2)}) copy-start(bf16[128,24,128]{2,1,0:T(8,128)(2,1)} %param.19) | copy-start | bytes 2359300
  7.2 33.7 %copy-start.19 = (bf16[128,24,128]{2,1,0:T(8,128)(2,1)S(1)}, bf16[128,24,128]{2,1,0:T(8,128)(2,1)}, u32[]{:S(2)}) copy-start(bf16[128,24,128]{2,1,0:T(8,128)(2,1)} %param.15) | copy-start | bytes 2359300
  7.2 70.3 %all-gather.5.cloned.1.call-start = ((), (), s32[]{:S(2)}) async-start(), calls=%async_computation.4 | async-start | bytes 4325376 | tf_op jit(solution)/shard_map/all_gather | solution.py:125
  8.9 132.2 %all-gather.7.cloned.1.call-start = ((), (), s32[]{:S(2)}) async-start(), calls=%async_computation.5 | async-start | bytes 4325376 | tf_op jit(solution)/shard_map/all_gather | solution.py:128
  10.6 191.5 %all-gather.9.cloned.1.call-start = ((), (), s32[]{:S(2)}) async-start(), calls=%async_computation.6 | async-start | bytes 2162688 | tf_op jit(solution)/shard_map/all_gather | solution.py:133
  11.5 12.1 %collective-permute-start = (bf16[64,4,128]{2,0,1:T(8,128)(2,1)S(1)}, bf16[64,4,128]{2,0,1:T(8,128)(2,1)S(1)}, u32[]{:S(2)}, u32[]{:S(2)}) collective-permute-start(bf16[64,4,128]{2,0,1:T(8,128)(2,1)S(1)} %slice.116), channel_id=1, source_target_pairs={{0,32},{32,64},{64,96},{96,128},{128,160},{160,192},{192,224},{1,3... | collective-permute-start | bytes 196616 | tf_op jit(solution)/shard_map/ppermute | solution.py:12
  24.3 238.7 %all-gather.11.cloned.1.call-start = ((), (), s32[]{:S(2)}) async-start(), calls=%async_computation.7 | async-start | bytes 2162688 | tf_op jit(solution)/shard_map/all_gather | solution.py:134
  25.2 12.3 %collective-permute-start.1 = (bf16[64,4,128]{2,0,1:T(8,128)(2,1)S(1)}, bf16[64,4,128]{2,0,1:T(8,128)(2,1)S(1)}, u32[]{:S(2)}, u32[]{:S(2)}) collective-permute-start(bf16[64,4,128]{2,0,1:T(8,128)(2,1)S(1)} %slice.117), channel_id=1, source_target_pairs={{0,32},{32,64},{64,96},{96,128},{128,160},{160,192},{192,224},{1,3... | collective-permute-start | bytes 196616 | tf_op jit(solution)/shard_map/ppermute | solution.py:12
  38.1 499.5 %reduce-scatter.7.cloned.1.call-start = ((), (), s32[]{:S(2)}) async-start(), calls=%async_computation.9 | async-start | bytes 2162688 | tf_op jit(solution)/shard_map/reduce_scatter | solution.py:216
  271.3 3.7 copy-start
  282.4 5.1 copy-start.29
  295.1 5.7 copy-start.13
  301.4 3.3 copy-start.10
  301.4 3.3 copy-start.27
  304.7 3.7 copy-start
  324.0 5.7 copy-start.13
  330.2 3.2 copy-start.10
  330.2 3.2 copy-start.27
  333.5 3.7 copy-start
  352.7 5.7 copy-start.13
  359.0 3.2 copy-start.10
  362.2 3.7 copy-start
  381.4 5.6 copy-start.13
  387.7 3.3 copy-start.10
  387.7 3.3 copy-start.27
  391.0 293.2 %reduce-scatter.11.cloned.1.call-start = ((), (), s32[]{:S(2)}) async-start(), calls=%async_computation.11 | async-start | bytes 2162688 | tf_op jit(solution)/shard_map/reduce_scatter | solution.py:217
  391.6 442.2 %reduce-scatter.5.cloned.1.call-start = ((), (), s32[]{:S(2)}) async-start(), calls=%async_computation.8 | async-start | bytes 4325376 | tf_op jit(solution)/shard_map/reduce_scatter | solution.py:212
  392.3 150.4 %copy-start.11 = (f32[64,4,6,128]{3,0,2,1:T(8,128)S(1)}, f32[64,4,6,128]{3,0,2,1:T(8,128)}, u32[]{:S(2)}) copy-start(f32[64,4,6,128]{3,0,2,1:T(8,128)} %get-tuple-element.718) | copy-start | bytes 2359300
  392.4 150.4 %copy-start.14 = (f32[64,4,6,128]{3,0,2,1:T(8,128)S(1)}, f32[64,4,6,128]{3,0,2,1:T(8,128)}, u32[]{:S(2)}) copy-start(f32[64,4,6,128]{3,0,2,1:T(8,128)} %get-tuple-element.719) | copy-start | bytes 2359300
  392.4 591.1 %reduce-scatter.9.cloned.1.call-start = ((), (), s32[]{:S(2)}) async-start(), calls=%async_computation.10 | async-start | bytes 4325376 | tf_op jit(solution)/shard_map/reduce_scatter | solution.py:213
  537.6 297.0 %collective-permute-start.2 = (bf16[64,4,128]{2,0,1:T(8,128)(2,1)}, bf16[64,4,128]{2,0,1:T(8,128)(2,1)S(1)}, u32[]{:S(2)}, u32[]{:S(2)}) collective-permute-start(bf16[64,4,128]{2,0,1:T(8,128)(2,1)} %reduce-scatter.7.cloned.1.call-done), channel_id=1, source_target_pairs={{32,0},{64,32},{96,64},{128,96},{160,128},{192,160},{224,192},{33,... | collective-permute-start | bytes 196616 | tf_op jit(solution)/shard_map/ppermute | solution.py:12
  684.2 300.2 %collective-permute-start.3 = (bf16[64,4,128]{2,0,1:T(8,128)(2,1)}, bf16[64,4,128]{2,0,1:T(8,128)(2,1)S(1)}, u32[]{:S(2)}, u32[]{:S(2)}) collective-permute-start(bf16[64,4,128]{2,0,1:T(8,128)(2,1)} %reduce-scatter.11.cloned.1.call-done), channel_id=1, source_target_pairs={{32,0},{64,32},{96,64},{128,96},{160,128},{192,160},{224,192},{33,... | collective-permute-start | bytes 196616 | tf_op jit(solution)/shard_map/ppermute | solution.py:12
  (95 other events, 147.2 us)
Sparse Core Ops, SparseCore 0:
  10.5 66.9 all-gather.4
  79.9 61.2 all-gather.6
  143.0 58.9 all-gather.8
  203.8 59.0 all-gather.10
  391.1 146.4 reduce-scatter.6
  540.2 143.9 reduce-scatter.10
  686.7 147.0 reduce-scatter.4
  836.3 147.1 reduce-scatter.8
where the time goes:
time: 994 us; the launch traced here: 993 us
  waiting for transfers between devices  795 us (80%)
  local copies, waits for them, and re-layouts  67.8 us (7%)
  matrix products  66.2 us (7%)
  starting transfers between devices  27.8 us (3%)
  other arithmetic  19.8 us (2%)
  between operations  14.4 us (1%)
    reduce_scatter x1, waiting for transfers between devices, on_device(): lax.psum_scatter(own_values, 'inner', scatter_dimension=1, tiled=True)  147 us
    reduce_scatter x1, waiting for transfers between devices, on_device(): lax.psum_scatter(own_keys, 'inner', scatter_dimension=1, tiled=True)  145 us
    reduce_scatter x1, waiting for transfers between devices, on_device(): lax.psum_scatter(back_keys, 'inner', scatter_dimension=0, tiled=True)  145 us
    reduce_scatter x1, waiting for transfers between devices, on_device(): lax.psum_scatter(back_values, 'inner', scatter_dimension=0, tiled=True)  140 us
    all_gather x1, waiting for transfers between devices, on_device(): lax.all_gather(shifted[1], 'inner', axis=0, tiled=True)  60.9 us
    all_gather x1, waiting for transfers between devices, on_device(): lax.all_gather(value.reshape(2, part_rows, key_heads, head_width), 'inner...  59.3 us
    all_gather x1, waiting for transfers between devices, on_device(): lax.all_gather(shifted[0], 'inner', axis=0, tiled=True)  56.4 us
    all_gather x1, waiting for transfers between devices, on_device(): lax.all_gather(key.reshape(2, part_rows, key_heads, head_width), 'inner',...  33.4 us
  transfers between devices with their start and end apart: 12, of which 10 were waited for; matrix products, arithmetic and copies ran while one was open for 2% of the time, Pallas kernels for 0%

commit v1 on v0

v1 whole, which is shorter than its diff:
```python
import math

import jax
import jax.numpy as jnp
from jax import lax
from jax.experimental import pallas as pl
from jax.experimental.pallas import tpu as pltpu
from jax.sharding import PartitionSpec as P

MESH = pl.DeviceIdType.MESH
ZS, XS = 4, 4
KV, GROUP, DIM, BLK = 4, 6, 128, 64
ROWS = GROUP * BLK
WINDOWS = 8
WIN_BLOCKS = 64
WIN_ROWS = WIN_BLOCKS * BLK
PAD_PAIRS, PRIOR_PAIRS = 2, 12
BASE_PAIRS = PAD_PAIRS + PRIOR_PAIRS
PAIRS = BASE_PAIRS + WIN_BLOCKS // 2
KEY_ROWS = PAIRS * 2 * BLK
BASE_ROW = BASE_PAIRS * 2 * BLK
TILE = 256
SCALE = 1.0 / math.sqrt(DIM)
LOG2E = math.log2(math.e)

NEED = {
    0: (0, 4, 5, 2, 6, 3, 7, 8, 9, 10),
    1: (1, 5, 0, 2, 6, 3, 7, 8, 9, 10),
    2: (2, 6, 1, 3, 7, 0),
    3: (3, 7, 2, 1, 0),
}
PRIOR_FROM = (0, 1, 2)
PRIOR_TO = (0, 1)


def owner_z(gid):
    return gid % 4


def place():
    inner = lax.axis_index("inner")
    return lax.axis_index("outer"), inner // (2 * XS), (inner // 2) % XS, inner % 2


def device(window, z, x, core):
    return {"outer": window, "inner": (z * XS + x) * 2 + core}


def group_slot(gid, core):
    z = owner_z(gid)
    if gid < 4:
        return BASE_PAIRS + 4 * z, core
    if gid < 8:
        return BASE_PAIRS + 28 - 4 * z, 1 - core
    return PAD_PAIRS + 8 - 4 * z, 1 - core


def group_of(ref, gid, core):
    pair, parity = group_slot(gid, core)
    return ref.at[:, pl.ds(pair, 4), parity]


def block_of(ref, half, z, x, core):
    if half == 0:
        return ref.at[:, BASE_PAIRS + 4 * z + x, core]
    return ref.at[:, BASE_PAIRS + 31 - 4 * z - x, 1 - core]


def has_next(window, z):
    return (window < WINDOWS - 1) & (z <= 2)


def has_previous(window, z):
    return (window > 0) & (z <= 1)


def greet(window, z, x, core):
    barrier = pltpu.get_barrier_semaphore()

    def signal(*where):
        pl.semaphore_signal(barrier, inc=1, device_id=device(*where), device_id_type=MESH)

    for step in range(1, XS):
        signal(window, z, (x + step) % XS, core)
    for step in range(1, ZS):
        signal(window, (z + step) % ZS, x, core)
    signal(window, z, x, 1 - core)

    @pl.when(has_next(window, z))
    def _():
        for other in PRIOR_TO:
            signal(window + 1, other, x, core)

    @pl.when(has_previous(window, z))
    def _():
        for other in PRIOR_FROM:
            signal(window - 1, other, x, core)

    count = 7 + jnp.where(has_next(window, z), 2, 0) + jnp.where(has_previous(window, z), 3, 0)
    pl.semaphore_wait(barrier, count)


def remote(src, dst, send, recv, where):
    return pltpu.make_async_remote_copy(
        src_ref=src, dst_ref=dst, send_sem=send, recv_sem=recv, device_id=where, device_id_type=MESH
    )


def spread_kernel(
    kv_src, qd_src, ld_src, kv, qd, ld,
    kv_send, kv_recv, qd_send, qd_recv, ld_send, ld_recv,
    z_send, z_recv, next_send, next_recv, core_send, core_recv, own_sem,
):
    window, z, x, core = place()
    greet(window, z, x, core)

    def kv_copy(step, half):
        to = (x + step) % XS
        return remote(
            kv_src.at[to, :, half], block_of(kv, half, z, x, core),
            kv_send.at[step - 1, half], kv_recv.at[step - 1, half], device(window, z, to, core),
        )

    def kv_arrival(step, half):
        came = (x - step + XS) % XS
        return remote(
            kv_src.at[came, :, half], block_of(kv, half, z, came, core),
            kv_send.at[step - 1, half], kv_recv.at[step - 1, half], device(window, z, came, core),
        )

    def wide_copy(src, dst, send, recv, step):
        to = (x + step) % XS
        return remote(src.at[to], dst.at[x], send.at[step - 1], recv.at[step - 1], device(window, z, to, core))

    def wide_arrival(src, dst, send, recv, step):
        came = (x - step + XS) % XS
        return remote(
            src.at[came], dst.at[came], send.at[step - 1], recv.at[step - 1], device(window, z, came, core)
        )

    for step in (2, 1, 3):
        for half in (0, 1):
            kv_copy(step, half).start()
    own = [
        pltpu.make_async_copy(kv_src.at[x, :, half], block_of(kv, half, z, x, core), own_sem.at[half])
        for half in (0, 1)
    ]
    own += [
        pltpu.make_async_copy(qd_src.at[x], qd.at[x], own_sem.at[2]),
        pltpu.make_async_copy(ld_src.at[x], ld.at[x], own_sem.at[3]),
    ]
    for copy in own:
        copy.start()
    for step in (2, 1, 3):
        wide_copy(ld_src, ld, ld_send, ld_recv, step).start()
        wide_copy(qd_src, qd, qd_send, qd_recv, step).start()
    for copy in own:
        copy.wait()
    for step in (2, 1, 3):
        for half in (0, 1):
            kv_arrival(step, half).wait_recv()

    def z_copy(gid, to):
        piece = group_of(kv, gid, core)
        return remote(
            piece, piece, z_send.at[to, gid // 4], z_recv.at[gid], device(window, to, x, core)
        )

    def next_copy(gid, to):
        return remote(
            group_of(kv, gid - 4, core), group_of(kv, gid, core),
            next_send.at[to], next_recv.at[gid - 8], device(window + 1, to, x, core),
        )

    def next_arrival(gid):
        piece = group_of(kv, gid, core)
        return remote(piece, piece, next_send.at[0], next_recv.at[gid - 8], device(window, z, x, 1 - core))

    def core_copy(gid):
        piece = group_of(kv, gid, core)
        return remote(piece, piece, core_send.at[gid], core_recv.at[gid], device(window, z, x, 1 - core))

    def core_arrival(gid):
        piece = group_of(kv, gid, 1 - core)
        return remote(piece, piece, core_send.at[gid], core_recv.at[gid], device(window, z, x, 1 - core))

    def level(at):
        mine = (at, at + 4)
        near = [gid for gid in NEED[at] if gid < 8 and gid not in mine]
        far = [gid for gid in NEED[at] if gid >= 8]
        sends = [
            (gid, to) for to in (0, 3, 1, 2) for gid in mine if to != at and gid in NEED[to]
        ]
        for gid, to in sends:
            z_copy(gid, to).start()
        if at in PRIOR_FROM:

            @pl.when(window < WINDOWS - 1)
            def _():
                for to in PRIOR_TO:
                    next_copy(at + 8, to).start()

        for gid in mine:
            core_copy(gid).start()
        for gid in near:
            z_copy(gid, (owner_z(gid))).wait_recv()
            core_copy(gid).start()
        if far:

            @pl.when(window > 0)
            def _():
                for gid in far:
                    next_arrival(gid).wait_recv()
                    core_copy(gid).start()
                for gid in far:
                    core_arrival(gid).wait_recv()
                    core_copy(gid).wait_send()

        for gid in (*mine, *near):
            core_arrival(gid).wait_recv()
            core_copy(gid).wait_send()
        for gid, to in sends:
            z_copy(gid, to).wait_send()
        if at in PRIOR_FROM:

            @pl.when(window < WINDOWS - 1)
            def _():
                for to in PRIOR_TO:
                    next_copy(at + 8, to).wait_send()

    for at in range(ZS):
        pl.when(z == at)(lambda at=at: level(at))

    for step in (1, 2, 3):
        for half in (0, 1):
            kv_copy(step, half).wait_send()
        wide_arrival(ld_src, ld, ld_send, ld_recv, step).wait_recv()
        wide_arrival(qd_src, qd, qd_send, qd_recv, step).wait_recv()
        wide_copy(ld_src, ld, ld_send, ld_recv, step).wait_send()
        wide_copy(qd_src, qd, qd_send, qd_recv, step).wait_send()


def spread(kv_src, qd_src, ld_src):
    dma = pltpu.SemaphoreType.DMA
    anywhere = pl.BlockSpec(memory_space=pl.ANY)
    return pl.pallas_call(
        spread_kernel,
        out_shape=(
            jax.ShapeDtypeStruct((2, PAIRS, 2, BLK, DIM), jnp.bfloat16),
            jax.ShapeDtypeStruct(qd_src.shape, jnp.bfloat16),
            jax.ShapeDtypeStruct(ld_src.shape, jnp.float32),
        ),
        in_specs=[anywhere] * 3,
        out_specs=[anywhere] * 3,
        scratch_shapes=[
            dma((3, 2)), dma((3, 2)), dma((3,)), dma((3,)), dma((3,)), dma((3,)),
            dma((ZS, 2)), dma((8,)), dma((2,)), dma((3,)), dma((11,)), dma((11,)), dma((4,)),
        ],
        compiler_params=pltpu.CompilerParams(collective_id=0, has_side_effects=True),
        name="spread",
    )(kv_src, qd_src, ld_src)


def grads_kernel(info, starts, qd, ld, kv_hbm, dq, parts, kv, totals, dq_t, kv_sem):
    src, half = pl.program_id(0), pl.program_id(1)
    window, z, core = info[0], info[1], info[2]

    @pl.when((src == 0) & (half == 0))
    def _():
        load = pltpu.make_async_copy(kv_hbm, kv, kv_sem)
        load.start()
        totals[...] = jnp.zeros_like(totals)
        load.wait()

        def clear(first, blocks):
            kv[:, pl.ds(first * BLK, blocks * BLK), :] = jnp.zeros((2, blocks * BLK, DIM), jnp.bfloat16)

        clear(0, 2 * PAD_PAIRS)
        pl.when((z >= 2) | (window == 0))(lambda: clear(2 * PAD_PAIRS, 2 * PRIOR_PAIRS))
        pl.when(z == 0)(lambda: clear(2 * BASE_PAIRS + 8, 8))

    low = 8 * z + 2 * src + core
    block = jnp.where(half == 0, low, WIN_BLOCKS - 1 - low)
    shift = BASE_ROW - window * WIN_ROWS
    first = BASE_ROW + block * BLK
    query_row = first + (lax.broadcasted_iota(jnp.int32, (1, ROWS), 1) & (BLK - 1))
    query_from = jnp.zeros((1, ROWS), jnp.int32)
    begin = 0
    for entry in range(24):
        at = starts[entry] + shift
        query_from = jnp.where(query_row >= at, at, query_from)
        begin = jnp.where(first >= at, at, begin)
    end = first + BLK
    steps = (end - begin + TILE - 1) // TILE
    q, do = qd[0], qd[1]
    lse, delta = ld[pl.ds(2 * half, 1), :], ld[pl.ds(2 * half + 1, 1), :]
    dq_t[...] = jnp.zeros_like(dq_t)

    @pl.loop(0, steps)
    def _(step):
        row = pl.multiple_of(end - (step + 1) * TILE, BLK)
        rows = pl.ds(row, TILE)
        k, v = kv[0, rows, :], kv[1, rows, :]
        s = lax.dot_general(k, q, (((1,), (1,)), ((), ())), preferred_element_type=jnp.float32)
        dp = lax.dot_general(v, do, (((1,), (1,)), ((), ())), preferred_element_type=jnp.float32)
        key_row = row + lax.broadcasted_iota(jnp.int32, (TILE, 1), 0)
        allowed = (key_row <= query_row) & (key_row >= query_from)
        p = jnp.where(allowed, jnp.exp2(s * (SCALE * LOG2E) - lse), 0.0)
        ds = (p * (dp - delta)).astype(jnp.bfloat16)
        totals[1, rows, :] += jnp.dot(p.astype(jnp.bfloat16), do, preferred_element_type=jnp.float32)
        totals[0, rows, :] += jnp.dot(ds, q, preferred_element_type=jnp.float32)
        dq_t[...] += lax.dot_general(k, ds, (((0,), (0,)), ((), ())), preferred_element_type=jnp.float32)

    dq[...] = (dq_t[...].T * SCALE).astype(jnp.bfloat16)

    @pl.when((src == XS - 1) & (half == 1))
    def _():
        parts[0] = (totals[0] * SCALE).astype(jnp.bfloat16)
        parts[1] = totals[1].astype(jnp.bfloat16)


def grads(info, starts, qd, ld, kv):
    return pl.pallas_call(
        grads_kernel,
        grid_spec=pltpu.PrefetchScalarGridSpec(
            num_scalar_prefetch=2,
            grid=(XS, 2),
            in_specs=[
                pl.BlockSpec((None, 2, None, ROWS, DIM), lambda s, h, *_: (s, 0, h, 0, 0)),
                pl.BlockSpec((None, 8, ROWS), lambda s, h, *_: (s, 0, 0)),
                pl.BlockSpec(memory_space=pl.ANY),
            ],
            out_specs=[
                pl.BlockSpec((None, None, ROWS, DIM), lambda s, h, *_: (s, h, 0, 0)),
                pl.BlockSpec((2, KEY_ROWS, DIM), lambda s, h, *_: (0, 0, 0)),
            ],
            scratch_shapes=[
                pltpu.VMEM((2, KEY_ROWS, DIM), jnp.bfloat16),
                pltpu.VMEM((2, KEY_ROWS, DIM), jnp.float32),
                pltpu.VMEM((DIM, ROWS), jnp.float32),
                pltpu.SemaphoreType.DMA,
            ],
        ),
        out_shape=(
            jax.ShapeDtypeStruct((XS, 2, ROWS, DIM), jnp.bfloat16),
            jax.ShapeDtypeStruct((2, KEY_ROWS, DIM), jnp.bfloat16),
        ),
        compiler_params=pltpu.CompilerParams(
            dimension_semantics=("arbitrary", "arbitrary"), vmem_limit_bytes=40 * 2**20
        ),
        name="grads",
    )(info, starts, qd, ld, kv)


def collect_kernel(
    dq_src, parts, dq, dkv, own, sib, stage, near, far, final,
    dq_send, dq_recv, own_sem, core_send, core_recv, z_send, z_recv, next_send, next_recv,
    out_send, out_recv, last_sem,
):
    window, z, x, core = place()
    greet(window, z, x, core)

    def core_copy(gid):
        return remote(
            group_of(parts, gid, 1 - core), sib.at[gid],
            core_send.at[gid], core_recv.at[gid], device(window, z, x, 1 - core),
        )

    def own_copy(gid):
        return pltpu.make_async_copy(group_of(parts, gid, core), own.at[gid], own_sem.at[gid])

    def dq_copy(step):
        to = (x + step) % XS
        return remote(
            dq_src.at[to], dq.at[x], dq_send.at[step - 1], dq_recv.at[step - 1], device(window, z, to, core)
        )

    def dq_arrival(step):
        came = (x - step + XS) % XS
        return remote(
            dq_src.at[came], dq.at[came], dq_send.at[step - 1], dq_recv.at[step - 1],
            device(window, z, came, core),
        )

    dq_own = pltpu.make_async_copy(dq_src.at[x], dq.at[x], last_sem.at[0])

    def z_copy(gid, at):
        return remote(
            stage.at[gid], near.at[gid // 4, at], z_send.at[gid], z_recv.at[gid // 4, at],
            device(window, owner_z(gid), x, core),
        )

    def z_arrival(half, came):
        return remote(
            stage.at[0], near.at[half, came], z_send.at[0], z_recv.at[half, came],
            device(window, came, x, core),
        )

    def next_copy(gid, at):
        return remote(
            stage.at[gid], far.at[at], next_send.at[gid - 8], next_recv.at[at],
            device(window - 1, owner_z(gid), x, core),
        )

    def next_arrival(came):
        return remote(
            stage.at[0], far.at[came], next_send.at[0], next_recv.at[came],
            device(window, z, x, 1 - core),
        )

    def both(gid):
        return own[gid].astype(jnp.float32) + sib[gid].astype(jnp.float32)

    def level(at):
        mine = (at, at + 4)
        others = [gid for gid in reversed(NEED[at]) if gid < 8 and gid not in mine]
        previous = [gid for gid in NEED[at] if gid >= 8]
        order = (*others, *mine)

        if previous:

            @pl.when(window > 0)
            def _():
                for gid in previous:
                    core_copy(gid).start()
                    own_copy(gid).start()

        for gid in order:
            core_copy(gid).start()
            own_copy(gid).start()
        dq_own.start()
        for step in (2, 1, 3):
            dq_copy(step).start()

        if previous:

            @pl.when(window > 0)
            def _():
                for gid in previous:
                    own_copy(gid).wait()
                    core_copy(gid).wait_recv()
                    stage[gid] = both(gid).astype(jnp.bfloat16)
                    next_copy(gid, at).start()

        for gid in others:
            own_copy(gid).wait()
            core_copy(gid).wait_recv()
            stage[gid] = both(gid).astype(jnp.bfloat16)
            z_copy(gid, at).start()
        for gid in mine:
            half = gid // 4
            own_copy(gid).wait()
            core_copy(gid).wait_recv()
            total = both(gid)
            for came in range(ZS):
                if came != at and gid in NEED[came]:
                    z_arrival(half, came).wait_recv()
                    total = total + near[half, came].astype(jnp.float32)
            if half == 0 or at not in PRIOR_FROM:
                final[half] = total.astype(jnp.bfloat16)
            else:

                @pl.when(window < WINDOWS - 1)
                def _():
                    more = total
                    for came in PRIOR_TO:
                        next_arrival(came).wait_recv()
                        more = more + far[came].astype(jnp.float32)
                    final[half] = more.astype(jnp.bfloat16)

                @pl.when(window == WINDOWS - 1)
                def _():
                    final[half] = total.astype(jnp.bfloat16)

        for gid in order:
            core_copy(gid).wait_send()
        for gid in others:
            z_copy(gid, at).wait_send()
        if previous:

            @pl.when(window > 0)
            def _():
                for gid in previous:
                    core_copy(gid).wait_send()
                    next_copy(gid, at).wait_send()

    for at in range(ZS):
        pl.when(z == at)(lambda at=at: level(at))

    def piece(half, to):
        return final.at[half, :, to if half == 0 else 3 - to]

    def out_copy(step, half):
        to = (x + step) % XS
        return remote(
            piece(half, to), dkv.at[x, :, half],
            out_send.at[step - 1, half], out_recv.at[step - 1, half], device(window, z, to, core),
        )

    def out_arrival(step, half):
        came = (x - step + XS) % XS
        return remote(
            piece(half, came), dkv.at[came, :, half],
            out_send.at[step - 1, half], out_recv.at[step - 1, half], device(window, z, came, core),
        )

    for step in (2, 1, 3):
        for half in (0, 1):
            out_copy(step, half).start()
    out_own = [
        pltpu.make_async_copy(piece(half, x), dkv.at[x, :, half], last_sem.at[1 + half]) for half in (0, 1)
    ]
    for copy in out_own:
        copy.start()
    dq_own.wait()
    for copy in out_own:
        copy.wait()
    for step in (1, 2, 3):
        dq_arrival(step).wait_recv()
        dq_copy(step).wait_send()
        for half in (0, 1):
            out_arrival(step, half).wait_recv()
            out_copy(step, half).wait_send()


def collect(dq_src, parts):
    dma = pltpu.SemaphoreType.DMA
    anywhere = pl.BlockSpec(memory_space=pl.ANY)
    piece = (2, 4, BLK, DIM)
    return pl.pallas_call(
        collect_kernel,
        out_shape=(
            jax.ShapeDtypeStruct(dq_src.shape, jnp.bfloat16),
            jax.ShapeDtypeStruct((XS, 2, 2, BLK, DIM), jnp.bfloat16),
        ),
        in_specs=[anywhere] * 2,
        out_specs=[anywhere] * 2,
        scratch_shapes=[
            pltpu.VMEM((11, *piece), jnp.bfloat16),
            pltpu.VMEM((11, *piece), jnp.bfloat16),
            pltpu.VMEM((11, *piece), jnp.bfloat16),
            pltpu.VMEM((2, ZS, *piece), jnp.bfloat16),
            pltpu.VMEM((2, *piece), jnp.bfloat16),
            pltpu.VMEM((2, *piece), jnp.bfloat16),
            dma((3,)), dma((3,)), dma((11,)), dma((11,)), dma((11,)), dma((8,)), dma((2, ZS)),
            dma((3,)), dma((2,)), dma((3, 2)), dma((3, 2)), dma((3,)),
        ],
        compiler_params=pltpu.CompilerParams(
            collective_id=1, has_side_effects=True, vmem_limit_bytes=32 * 2**20
        ),
        name="collect",
    )(dq_src, parts)


def by_head(rows):
    cut = rows.reshape(2, BLK, KV, GROUP, DIM).transpose(2, 0, 3, 1, 4)
    return cut.reshape(KV, 2, ROWS, DIM)


def lanes(rows):
    return rows.reshape(KV, GROUP, 2, BLK).transpose(0, 2, 1, 3).reshape(KV, 2, ROWS)


def on_device(query, key, value, output, grad_output, lse, doc_starts):
    window, z, _, core = place()
    delta = jnp.einsum("qhd,qhd->hq", grad_output, output, preferred_element_type=jnp.float32)
    rows = jnp.stack([lanes(lse * LOG2E), lanes(delta)], axis=2).reshape(KV, 4, ROWS)
    ld_src = jnp.concatenate([rows, jnp.zeros_like(rows)], axis=1)
    qd_src = jnp.stack([by_head(query), by_head(grad_output)], axis=1)
    kv_src = jnp.stack([key, value]).reshape(2, 2, BLK, KV, DIM).transpose(3, 0, 1, 2, 4)
    kv, qd, ld = spread(kv_src, qd_src, ld_src)
    info = jnp.stack([window, z, core]).astype(jnp.int32)
    dq, parts = grads(info, doc_starts, qd, ld, kv.reshape(2, KEY_ROWS, DIM))
    dq_back, dkv = collect(dq, parts.reshape(2, PAIRS, 2, BLK, DIM))
    grad_query = (
        dq_back.reshape(KV, 2, GROUP, BLK, DIM).transpose(1, 3, 0, 2, 4).reshape(2 * BLK, KV * GROUP, DIM)
    )
    back = dkv.transpose(1, 2, 3, 0, 4).reshape(2, 2 * BLK, KV, DIM)
    return grad_query, back[0], back[1]


def solution(mesh):
    tokens = P(("outer", "inner"), None, None)
    return jax.shard_map(
        on_device,
        mesh=mesh,
        in_specs=(tokens, tokens, tokens, tokens, tokens, P(None, ("outer", "inner")), P()),
        out_specs=(tokens, tokens, tokens),
        check_vma=False,
    )
```

time: 994 us -> 135 us (0.14)
  the two profiles are of different devices: /device:TPU:16 before, /device:TPU:88 now
where the time goes in v1:
time: 135 us; the launch traced here: 134 us
  Pallas kernels  119 us (88%)
  local copies, waits for them, and re-layouts  9.52 us (7%)
  other arithmetic  4.74 us (4%)
    pallas_call x1, Pallas kernels, collect(): pl.pallas_call(collect_kernel, out_shape=(jax.ShapeDtypeStruct(dq_src.sha...  64 us
    pallas_call x1, Pallas kernels, spread(): pl.pallas_call(spread_kernel, out_shape=(jax.ShapeDtypeStruct((2, PAIRS,...  43.2 us
    pallas_call x1, Pallas kernels, grads(): pl.pallas_call(grads_kernel, grid_spec=pltpu.PrefetchScalarGridSpec(num_s...  12 us
    unnamed x23, local copies, waits for them, and re-layouts  8.23 us

profile of v1, /device:TPU:88, one launch (start us, length us, event | category | flops | bytes accessed | tf_op | source)
XLA Modules:
  0.0 134.3 jit_solution(5636701164921214159)
XLA Ops:
  0.6 0.0 copy-start.7
  0.6 0.0 copy-start.6
  0.7 0.1 pad_add_fusion.info
  0.7 0.7 broadcast_multiply_fusion
  1.5 0.1 reshape.45
  1.6 0.1 stack_reshape.14
  1.6 1.9 %fusion = f32[24,128]{0,1:T(8,128)S(1)} fusion(bf16[128,24,128]{2,1,0:T(8,128)(2,1)} %param.10, bf16[128,24,128]{2,1,0:T(8,128)(2,1)} %param.11), kind=kLoop, calls=%fused_computation.2 | loop fusion | flops 1569792 | bytes 1585152
  3.6 0.1 copy.37
  3.6 0.1 reshape.46
  3.8 0.1 stack_reshape.15
  3.9 0.6 concatenate.4.ld_src
  4.5 0.0 copy-done.6
  4.6 0.0 copy-done.7
  4.6 0.7 maximum_bitcast_fusion.kv_src
  5.3 0.2 copy.20
  5.5 0.1 copy.21
  5.6 0.9 copy-done.4
  6.5 0.2 copy.22
  6.6 0.1 copy.23
  6.7 1.3 pad_maximum_fusion.qd_src
  8.0 43.2 %spread.1 = (bf16[2,46,2,64,128]{4,3,2,1,0:T(8,128)(2,1)}, bf16[4,2,2,384,128]{4,3,2,1,0:T(8,128)(2,1)}, f32[4,8,384]{2,1,0:T(8,128)}) custom-call(bf16[4,2,2,64,128]{4,3,2,1,0:T(8,128)(2,1)} %maximum_bitcast_fusion.kv_src, bf16[4,2,2,384,128]{4,3,2,1,0:T(8,128)(2,1)} %pad_maximum_fusion.qd_src, f32[4,8,384]{2,1,0:T(8,128)} %concatenate.4.ld_src), custom_call_target="tpu_custom_call" | custom-call | tf_op jit(solution)/shard_map/spread/pallas_call | solution.py:246
  51.2 0.0 copy-done.3
  51.2 0.0 copy-start
  51.2 1.8 %copy-done = bf16[2,46,2,64,128]{4,3,2,1,0:T(8,128)(2,1)S(1)} copy-done((bf16[2,46,2,64,128]{4,3,2,1,0:T(8,128)(2,1)S(1)}, bf16[2,46,2,64,128]{4,3,2,1,0:T(8,128)(2,1)}, u32[]{:S(2)}) %copy-start) | copy-done | bytes 3014680
  53.1 1.4 %copy-done.1 = bf16[4,2,2,384,128]{4,3,2,1,0:T(8,128)(2,1)S(1)} copy-done((bf16[4,2,2,384,128]{4,3,2,1,0:T(8,128)(2,1)S(1)}, bf16[4,2,2,384,128]{4,3,2,1,0:T(8,128)(2,1)}, u32[]{:S(2)}) %copy-start.1) | copy-done | bytes 1572888
  54.5 0.8 copy-done.2
  55.3 12.0 %grads.1 = (bf16[4,2,384,128]{3,2,1,0:T(8,128)(2,1)S(1)}, bf16[2,5888,128]{2,1,0:T(8,128)(2,1)S(1)}) custom-call(s32[3]{0:T(128)S(1)} %pad_add_fusion.info, s32[24]{0:T(128)S(1)} %copy-done.3, bf16[4,2,2,384,128]{4,3,2,1,0:T(8,128)(2,1)S(1)} %copy-done.1, f32[4,8,384]{2,1,0:T(8,128)S(1)} %copy-done.2, bf16[2,5888,128]{2,1,0:T(8,128)(2,1)S(1)} %bitcast.32), custom_call_target="tpu_custom_call" | custom-call | tf_op jit(solution)/shard_map/grads/pallas_call | solution.py:323
  67.3 64.0 %collect.1 = (bf16[4,2,384,128]{3,2,1,0:T(8,128)(2,1)S(1)}, bf16[4,2,2,64,128]{4,3,2,1,0:T(8,128)(2,1)S(1)}) custom-call(bf16[4,2,384,128]{3,2,1,0:T(8,128)(2,1)S(1)} %get-tuple-element.13.dq_src, bf16[2,46,2,64,128]{4,3,2,1,0:T(8,128)(2,1)S(1)} %bitcast.33), custom_call_target="tpu_custom_call" | custom-call | tf_op jit(solution)/shard_map/collect/pallas_call | solution.py:530
  131.3 0.1 copy.27
  131.4 1.4 %copy.28 = bf16[128,24,128]{2,1,0:T(8,128)(2,1)} copy(bf16[128,24,128]{2,0,1:T(8,128)(2,1)S(1)} %bitcast.36) | data formatting | bytes 1572864
  132.8 0.8 copy.30
  133.6 0.8 copy.29
  (14 shorter events, 0.1 us)
Async XLA Ops:
  0.6 3.9 %copy-start.7 = (bf16[128,4,128]{2,1,0:T(4,128)(2,1)S(1)}, bf16[128,4,128]{2,1,0:T(4,128)(2,1)}, u32[]{:S(2)}) copy-start(bf16[128,4,128]{2,1,0:T(4,128)(2,1)} %param.9) | copy-start | bytes 393220
  0.6 3.9 %copy-start.6 = (bf16[128,4,128]{2,1,0:T(4,128)(2,1)S(1)}, bf16[128,4,128]{2,1,0:T(4,128)(2,1)}, u32[]{:S(2)}) copy-start(bf16[128,4,128]{2,1,0:T(4,128)(2,1)} %param.8) | copy-start | bytes 393220
  1.6 3.7 %copy-start.5 = (bf16[128,24,128]{2,1,0:T(8,128)(2,1)S(1)}, bf16[128,24,128]{2,1,0:T(8,128)(2,1)}, u32[]{:S(2)}) copy-start(bf16[128,24,128]{2,1,0:T(8,128)(2,1)} %param.7) | copy-start | bytes 2359300
  5.3 1.1 copy-start.4
  8.0 43.2 %copy-start.3 = (s32[24]{0:T(128)S(1)}, s32[24]{0:T(128)}, u32[]{:S(2)}) copy-start(s32[24]{0:T(128)} %starts.1) | copy-start | bytes 292
  51.2 1.9 %copy-start = (bf16[2,46,2,64,128]{4,3,2,1,0:T(8,128)(2,1)S(1)}, bf16[2,46,2,64,128]{4,3,2,1,0:T(8,128)(2,1)}, u32[]{:S(2)}) copy-start(bf16[2,46,2,64,128]{4,3,2,1,0:T(8,128)(2,1)} %get-tuple-element.12) | copy-start | bytes 9043972
  53.1 1.4 %copy-start.1 = (bf16[4,2,2,384,128]{4,3,2,1,0:T(8,128)(2,1)S(1)}, bf16[4,2,2,384,128]{4,3,2,1,0:T(8,128)(2,1)}, u32[]{:S(2)}) copy-start(bf16[4,2,2,384,128]{4,3,2,1,0:T(8,128)(2,1)} %get-tuple-element.10.qd) | copy-start | bytes 4718596
  54.5 0.8 copy-start.2

commit v2 on v1

v2 whole, which is shorter than its diff:
```python
import math

import jax
import jax.numpy as jnp
from jax import lax
from jax.experimental import pallas as pl
from jax.experimental.pallas import tpu as pltpu
from jax.sharding import PartitionSpec as P

MESH = pl.DeviceIdType.MESH
ZS, XS = 4, 4
KV, GROUP, DIM, BLK = 4, 6, 128, 64
ROWS = GROUP * BLK
WINDOWS = 8
WIN_BLOCKS = 64
WIN_ROWS = WIN_BLOCKS * BLK
PAD_PAIRS, PRIOR_PAIRS = 2, 12
BASE_PAIRS = PAD_PAIRS + PRIOR_PAIRS
PAIRS = BASE_PAIRS + WIN_BLOCKS // 2
KEY_ROWS = PAIRS * 2 * BLK
BASE_ROW = BASE_PAIRS * 2 * BLK
TILE = 256
SCALE = 1.0 / math.sqrt(DIM)
LOG2E = math.log2(math.e)

NEED = {
    0: (0, 4, 5, 2, 6, 3, 7, 8, 9, 10),
    1: (1, 5, 0, 2, 6, 3, 7, 8, 9, 10),
    2: (2, 6, 1, 3, 7, 0),
    3: (3, 7, 2, 1, 0),
}
SPREAD_ORDER = {0: (10, 9, 8, 5, 6, 2, 7, 3), 1: (6, 0, 2, 7, 3, 10, 9, 8), 2: (7, 1, 3, 0), 3: (2, 1, 0)}
COLLECT_ORDER = {0: (7, 3, 6, 2, 5, 8, 9, 10), 1: (8, 9, 10, 7, 3, 6, 2, 0), 2: (0, 1, 7, 3), 3: (0, 1, 2)}
PRIOR_FROM = (0, 1, 2)


def owner_z(gid):
    return gid % 4


def place():
    inner = lax.axis_index("inner")
    return lax.axis_index("outer"), inner // (2 * XS), (inner // 2) % XS, inner % 2


def device(window, z, x, core):
    return {"outer": window, "inner": (z * XS + x) * 2 + core}


def piece_of(ref, gid, core, x):
    z = owner_z(gid)
    if gid < 4:
        return ref.at[:, BASE_PAIRS + 4 * z + x, core]
    if gid < 8:
        return ref.at[:, BASE_PAIRS + 31 - 4 * z - x, 1 - core]
    return ref.at[:, PAD_PAIRS + 11 - 4 * z - x, 1 - core]


def block_of(ref, half, z, x, core):
    if half == 0:
        return ref.at[:, BASE_PAIRS + 4 * z + x, core]
    return ref.at[:, BASE_PAIRS + 31 - 4 * z - x, 1 - core]


def turn(x, step):
    return (x + step + XS) % XS


def has_next(window, z):
    return (window < WINDOWS - 1) & (z <= 2)


def has_previous(window, z):
    return (window > 0) & (z == 0)


def greet(window, z, x, core):
    barrier = pltpu.get_barrier_semaphore()

    def signal(*where):
        pl.semaphore_signal(barrier, inc=1, device_id=device(*where), device_id_type=MESH)

    for step in range(1, XS):
        signal(window, z, (x + step) % XS, core)
    signal(window, z, x, 1 - core)
    pl.when(z > 0)(lambda: signal(window, z - 1, x, core))
    pl.when(z < ZS - 1)(lambda: signal(window, z + 1, x, core))
    pl.when(has_next(window, z))(lambda: signal(window + 1, 0, x, core))

    @pl.when(has_previous(window, z))
    def _():
        for other in PRIOR_FROM:
            signal(window - 1, other, x, core)

    count = 4 + jnp.where(z > 0, 1, 0) + jnp.where(z < ZS - 1, 1, 0)
    count = count + jnp.where(has_next(window, z), 1, 0) + jnp.where(has_previous(window, z), 3, 0)
    pl.semaphore_wait(barrier, count)


def remote(src, dst, send, recv, where):
    return pltpu.make_async_remote_copy(
        src_ref=src, dst_ref=dst, send_sem=send, recv_sem=recv, device_id=where, device_id_type=MESH
    )


def spread_kernel(
    kv_src, qd_src, ld_src, kv, qd, ld,
    kv_send, kv_recv, qd_send, qd_recv, ld_send, ld_recv,
    z_send, z_recv, next_send, next_recv, core_send, core_recv, own_sem,
):
    window, z, x, core = place()
    greet(window, z, x, core)

    def kv_copy(step, half):
        to = turn(x, step)
        return remote(
            kv_src.at[to, :, half], block_of(kv, half, z, x, core),
            kv_send.at[step, half], kv_recv.at[step, half], device(window, z, to, core),
        )

    def kv_arrival(step, half):
        came = turn(x, -step)
        return remote(
            kv_src.at[came, :, half], block_of(kv, half, z, came, core),
            kv_send.at[step, half], kv_recv.at[step, half], device(window, z, came, core),
        )

    def wide(src, dst, send, recv, step):
        to = turn(x, step)
        return remote(
            src.at[to], dst.at[step - 1], send.at[step - 1], recv.at[step - 1], device(window, z, to, core)
        )

    for step in (2, 1, 3):
        for half in (1, 0):
            kv_copy(step, half).start()
    own = [
        pltpu.make_async_copy(kv_src.at[x, :, half], block_of(kv, half, z, x, core), own_sem.at[half])
        for half in (0, 1)
    ]

    def z_copy(gid, j, at, way, src=None):
        piece = piece_of(kv, gid, core, turn(x, -j))
        return remote(
            piece if src is None else src, piece,
            z_send.at[gid, (way + 1) // 2, j], z_recv.at[gid, j], device(window, at + way, x, core),
        )

    def next_copy(gid, j, src=None):
        piece = piece_of(kv, gid, core, turn(x, -j))
        return remote(
            piece if src is None else src, piece_of(kv, gid + 4, core, turn(x, -j)),
            next_send.at[j], next_recv.at[gid - 4, j], device(window + 1, 0, x, core),
        )

    def next_arrival(gid, j):
        piece = piece_of(kv, gid, core, turn(x, -j))
        return remote(piece, piece, next_send.at[j], next_recv.at[gid - 8, j], device(window, z, x, 1 - core))

    def core_copy(gid, j, src=None):
        piece = piece_of(kv, gid, core, turn(x, -j))
        return remote(
            piece if src is None else src, piece,
            core_send.at[gid, j], core_recv.at[gid, j], device(window, z, x, 1 - core),
        )

    def core_arrival(gid, j):
        piece = piece_of(kv, gid, 1 - core, turn(x, -j))
        return remote(piece, piece, core_send.at[gid, j], core_recv.at[gid, j], device(window, z, x, 1 - core))

    def level(at):
        def ways(gid):
            owner = 0 if gid >= 8 else owner_z(gid)
            return [
                way
                for way in (-1, 1)
                if 0 <= at + way < ZS and gid in NEED[at + way] and abs(at + way - owner) > abs(at - owner)
            ]

        def onward(gid, j, src=None):
            for way in ways(gid):
                z_copy(gid, j, at, way, src).start()
            core_copy(gid, j, src).start()

        def guarded(gid, act):
            if gid >= 8:
                pl.when(window > 0)(act)
            else:
                act()

        def given(j, src=False):
            for gid in (at + 4, at):
                first = kv_src.at[x, :, gid // 4] if src else None
                if gid >= 4 and at in PRIOR_FROM:
                    pl.when(window < WINDOWS - 1)(lambda: next_copy(gid, j, first).start())
                onward(gid, j, first)

        def arrived(gid, j):
            if gid >= 8 and at == 0:
                next_arrival(gid, j).wait_recv()
            else:
                z_copy(gid, j, at, 1 if at < ZS - 1 else -1).wait_recv()
            onward(gid, j)

        given(0, True)
        for copy in own:
            copy.start()
        for step in (2, 1, 3):
            wide(ld_src, ld, ld_send, ld_recv, step).start()
            wide(qd_src, qd, qd_send, qd_recv, step).start()

        @pl.loop(1, XS)
        def _(j):
            for half in (0, 1):
                kv_arrival(j, half).wait_recv()
            given(j)

        for gid in SPREAD_ORDER[at]:
            guarded(gid, lambda: pl.loop(0, XS)(lambda j: arrived(gid, j)))

        @pl.loop(0, XS)
        def _(j):
            for gid in NEED[at]:

                def act():
                    core_arrival(gid, j).wait_recv()
                    core_copy(gid, j).wait_send()
                    for way in ways(gid):
                        z_copy(gid, j, at, way).wait_send()

                guarded(gid, act)
            if at in PRIOR_FROM:
                pl.when(window < WINDOWS - 1)(lambda: next_copy(at + 4, j).wait_send())

    for at in range(ZS):
        pl.when(z == at)(lambda at=at: level(at))

    for copy in own:
        copy.wait()
    for step in (1, 2, 3):
        for half in (0, 1):
            kv_copy(step, half).wait_send()
        wide(ld_src, ld, ld_send, ld_recv, step).wait()
        wide(qd_src, qd, qd_send, qd_recv, step).wait()


def spread(kv_src, qd_src, ld_src):
    dma = pltpu.SemaphoreType.DMA
    anywhere = pl.BlockSpec(memory_space=pl.ANY)
    return pl.pallas_call(
        spread_kernel,
        out_shape=(
            jax.ShapeDtypeStruct((2, PAIRS, 2, BLK, DIM), jnp.bfloat16),
            jax.ShapeDtypeStruct((XS - 1, *qd_src.shape[1:]), jnp.bfloat16),
            jax.ShapeDtypeStruct((XS - 1, *ld_src.shape[1:]), jnp.float32),
        ),
        in_specs=[anywhere] * 3,
        out_specs=[anywhere] * 3,
        scratch_shapes=[
            dma((XS, 2)), dma((XS, 2)), dma((3,)), dma((3,)), dma((3,)), dma((3,)),
            dma((11, 2, XS)), dma((11, XS)), dma((XS,)), dma((3, XS)), dma((11, XS)), dma((11, XS)), dma((2,)),
        ],
        compiler_params=pltpu.CompilerParams(collective_id=0, has_side_effects=True),
        name="spread",
    )(kv_src, qd_src, ld_src)


def grads_kernel(info, starts, qd_own, ld_own, qd, ld, kv_hbm, dq, parts, kv, totals, dq_t, kv_sem):
    step, half = pl.program_id(0), pl.program_id(1)
    window, z, core = info[0], info[1], info[2]
    src = (info[3] - step + XS) % XS

    @pl.when((step == 0) & (half == 0))
    def _():
        load = pltpu.make_async_copy(kv_hbm, kv, kv_sem)
        load.start()
        totals[...] = jnp.zeros_like(totals)
        load.wait()

        def clear(first, blocks):
            kv[:, pl.ds(first * BLK, blocks * BLK), :] = jnp.zeros((2, blocks * BLK, DIM), jnp.bfloat16)

        clear(0, 2 * PAD_PAIRS)
        pl.when((z >= 2) | (window == 0))(lambda: clear(2 * PAD_PAIRS, 2 * PRIOR_PAIRS))
        pl.when(z == 0)(lambda: clear(2 * BASE_PAIRS + 8, 8))

    low = 8 * z + 2 * src + core
    block = jnp.where(half == 0, low, WIN_BLOCKS - 1 - low)
    shift = BASE_ROW - window * WIN_ROWS
    first = BASE_ROW + block * BLK
    query_row = first + (lax.broadcasted_iota(jnp.int32, (1, ROWS), 1) & (BLK - 1))
    query_from = jnp.zeros((1, ROWS), jnp.int32)
    begin = 0
    for entry in range(24):
        at = starts[entry] + shift
        query_from = jnp.where(query_row >= at, at, query_from)
        begin = jnp.where(first >= at, at, begin)
    end = first + BLK
    tiles = (end - begin + TILE - 1) // TILE
    q = jnp.where(step == 0, qd_own[0], qd[0])
    do = jnp.where(step == 0, qd_own[1], qd[1])
    row_at = pl.ds(2 * half, 1)
    lse = jnp.where(step == 0, ld_own[row_at, :], ld[row_at, :])
    row_at = pl.ds(2 * half + 1, 1)
    delta = jnp.where(step == 0, ld_own[row_at, :], ld[row_at, :])
    dq_t[...] = jnp.zeros_like(dq_t)

    @pl.loop(0, tiles)
    def _(tile):
        row = pl.multiple_of(end - (tile + 1) * TILE, BLK)
        rows = pl.ds(row, TILE)
        k, v = kv[0, rows, :], kv[1, rows, :]
        s = lax.dot_general(k, q, (((1,), (1,)), ((), ())), preferred_element_type=jnp.float32)
        dp = lax.dot_general(v, do, (((1,), (1,)), ((), ())), preferred_element_type=jnp.float32)
        key_row = row + lax.broadcasted_iota(jnp.int32, (TILE, 1), 0)
        allowed = (key_row <= query_row) & (key_row >= query_from)
        p = jnp.where(allowed, jnp.exp2(s * (SCALE * LOG2E) - lse), 0.0)
        ds = (p * (dp - delta)).astype(jnp.bfloat16)
        totals[1, rows, :] += jnp.dot(p.astype(jnp.bfloat16), do, preferred_element_type=jnp.float32)
        totals[0, rows, :] += jnp.dot(ds, q, preferred_element_type=jnp.float32)
        dq_t[...] += lax.dot_general(k, ds, (((0,), (0,)), ((), ())), preferred_element_type=jnp.float32)

    dq[...] = (dq_t[...].T * SCALE).astype(jnp.bfloat16)

    @pl.when((step == XS - 1) & (half == 1))
    def _():
        parts[0] = (totals[0] * SCALE).astype(jnp.bfloat16)
        parts[1] = totals[1].astype(jnp.bfloat16)


def grads(info, starts, qd_own, ld_own, qd, ld, kv):
    return pl.pallas_call(
        grads_kernel,
        grid_spec=pltpu.PrefetchScalarGridSpec(
            num_scalar_prefetch=2,
            grid=(XS, 2),
            in_specs=[
                pl.BlockSpec(
                    (None, 2, None, ROWS, DIM),
                    lambda s, h, info, _: (info[3], 0, jnp.where(s == 0, h, 1), 0, 0),
                ),
                pl.BlockSpec((None, 8, ROWS), lambda s, h, info, _: (info[3], 0, 0)),
                pl.BlockSpec(
                    (None, 2, None, ROWS, DIM),
                    lambda s, h, *_: (jnp.maximum(s - 1, 0), 0, jnp.where(s == 0, 0, h), 0, 0),
                ),
                pl.BlockSpec((None, 8, ROWS), lambda s, h, *_: (jnp.maximum(s - 1, 0), 0, 0)),
                pl.BlockSpec(memory_space=pl.ANY),
            ],
            out_specs=[
                pl.BlockSpec((None, None, ROWS, DIM), lambda s, h, *_: (s, h, 0, 0)),
                pl.BlockSpec((2, KEY_ROWS, DIM), lambda s, h, *_: (0, 0, 0)),
            ],
            scratch_shapes=[
                pltpu.VMEM((2, KEY_ROWS, DIM), jnp.bfloat16),
                pltpu.VMEM((2, KEY_ROWS, DIM), jnp.float32),
                pltpu.VMEM((DIM, ROWS), jnp.float32),
                pltpu.SemaphoreType.DMA,
            ],
        ),
        out_shape=(
            jax.ShapeDtypeStruct((XS, 2, ROWS, DIM), jnp.bfloat16),
            jax.ShapeDtypeStruct((2, KEY_ROWS, DIM), jnp.bfloat16),
        ),
        compiler_params=pltpu.CompilerParams(
            dimension_semantics=("arbitrary", "arbitrary"), vmem_limit_bytes=40 * 2**20
        ),
        name="grads",
    )(info, starts, qd_own, ld_own, qd, ld, kv)


def collect_kernel(
    dq_src, parts, dq, dkv, own, sib, stage, near, far, final,
    dq_send, dq_recv, own_sem, core_send, core_recv, z_send, z_recv, next_send, next_recv,
    out_send, out_recv, last_sem,
):
    window, z, x, core = place()
    greet(window, z, x, core)

    def core_copy(gid, j):
        return remote(
            piece_of(parts, gid, 1 - core, turn(x, j + 1)), sib.at[gid, j],
            core_send.at[gid, j], core_recv.at[gid, j], device(window, z, x, 1 - core),
        )

    def own_copy(gid, j):
        return pltpu.make_async_copy(piece_of(parts, gid, core, turn(x, j + 1)), own.at[gid, j], own_sem.at[gid, j])

    def dq_copy(step):
        to = turn(x, -step)
        return remote(
            dq_src.at[step], dq.at[x], dq_send.at[step - 1], dq_recv.at[step - 1], device(window, z, to, core)
        )

    def dq_arrival(step):
        came = turn(x, step)
        return remote(
            dq_src.at[step], dq.at[came], dq_send.at[step - 1], dq_recv.at[step - 1],
            device(window, z, came, core),
        )

    def out_copy(half, j):
        return remote(
            final.at[half, j], dkv.at[x, :, half],
            out_send.at[half, j], out_recv.at[half, j], device(window, z, turn(x, j + 1), core),
        )

    def out_arrival(half, j):
        came = turn(x, -j - 1)
        return remote(
            final.at[half, j], dkv.at[came, :, half],
            out_send.at[half, j], out_recv.at[half, j], device(window, z, came, core),
        )

    def out_own(half):
        return pltpu.make_async_copy(final.at[half, XS - 1], dkv.at[x, :, half], last_sem.at[1 + half])

    dq_own = pltpu.make_async_copy(dq_src.at[0], dq.at[x], last_sem.at[0])

    def z_copy(gid, j, at, way):
        return remote(
            stage.at[gid, j], near.at[gid, (1 - way) // 2, j],
            z_send.at[gid, j], z_recv.at[gid, (1 - way) // 2, j], device(window, at + way, x, core),
        )

    def next_copy(gid, j):
        return remote(
            stage.at[gid, j], far.at[j], next_send.at[gid - 8, j], next_recv.at[j],
            device(window - 1, owner_z(gid), x, core),
        )

    def next_arrival(j):
        return remote(
            stage.at[8, j], far.at[j], next_send.at[0, j], next_recv.at[j], device(window, z, x, 1 - core),
        )

    def level(at):
        order = COLLECT_ORDER[at]
        mine = (at, at + 4)

        def each(gids, act, j):
            for gid in gids:
                if gid >= 8:
                    pl.when(window > 0)(lambda: act(gid, j))
                else:
                    act(gid, j)

        def begin(gid, j):
            core_copy(gid, j).start()
            own_copy(gid, j).start()

        def towards(gid):
            owner = 0 if gid >= 8 else owner_z(gid)
            return 1 if owner > at else -1

        def summed(gid, j):
            own_copy(gid, j).wait()
            core_copy(gid, j).wait_recv()
            total = own[gid, j].astype(jnp.float32) + sib[gid, j].astype(jnp.float32)
            owner = 0 if gid >= 8 else owner_z(gid)
            for way in (-1, 1):
                came = at + way
                if 0 <= came < ZS and gid in NEED[came] and abs(came - owner) > abs(at - owner):
                    z_copy(gid, j, came, -way).wait_recv()
                    total = total + near[gid, (way + 1) // 2, j].astype(jnp.float32)
            return total

        def pass_on(gid, j):
            stage[gid, j] = summed(gid, j).astype(jnp.bfloat16)
            if gid >= 8 and at == 0:
                next_copy(gid, j).start()
            else:
                z_copy(gid, j, at, towards(gid)).start()

        def keep(half, j):
            total = summed(mine[half], j)
            if half == 0 or at not in PRIOR_FROM:
                final[half, j] = total.astype(jnp.bfloat16)
            else:

                @pl.when(window < WINDOWS - 1)
                def _():
                    next_arrival(j).wait_recv()
                    final[half, j] = (total + far[j].astype(jnp.float32)).astype(jnp.bfloat16)

                @pl.when(window == WINDOWS - 1)
                def _():
                    final[half, j] = total.astype(jnp.bfloat16)

        def finish(gid, j):
            core_copy(gid, j).wait_send()
            if gid in mine:
                return
            if gid >= 8 and at == 0:
                next_copy(gid, j).wait_send()
            else:
                z_copy(gid, j, at, towards(gid)).wait_send()

        @pl.loop(0, XS)
        def _(j):
            each((*order, *mine), begin, j)

        dq_own.start()
        for step in (2, 1, 3):
            dq_copy(step).start()
        for gid in order:
            each([gid], lambda gid, _: pl.loop(0, XS)(lambda j: pass_on(gid, j)), None)
        for half in (0, 1):

            @pl.loop(0, XS - 1)
            def _(j):
                keep(half, j)
                out_copy(half, j).start()

            keep(half, XS - 1)
            out_own(half).start()

        @pl.loop(0, XS)
        def _(j):
            each((*order, *mine), finish, j)

    for at in range(ZS):
        pl.when(z == at)(lambda at=at: level(at))

    dq_own.wait()
    for half in (0, 1):
        out_own(half).wait()
    for step in (1, 2, 3):
        dq_arrival(step).wait_recv()
        dq_copy(step).wait_send()
        for half in (0, 1):
            out_arrival(half, step - 1).wait_recv()
            out_copy(half, step - 1).wait_send()


def collect(dq_src, parts):
    dma = pltpu.SemaphoreType.DMA
    anywhere = pl.BlockSpec(memory_space=pl.ANY)
    piece = (2, BLK, DIM)
    return pl.pallas_call(
        collect_kernel,
        out_shape=(
            jax.ShapeDtypeStruct(dq_src.shape, jnp.bfloat16),
            jax.ShapeDtypeStruct((XS, 2, 2, BLK, DIM), jnp.bfloat16),
        ),
        in_specs=[anywhere] * 2,
        out_specs=[anywhere] * 2,
        scratch_shapes=[
            pltpu.VMEM((11, XS, *piece), jnp.bfloat16),
            pltpu.VMEM((11, XS, *piece), jnp.bfloat16),
            pltpu.VMEM((11, XS, *piece), jnp.bfloat16),
            pltpu.VMEM((11, 2, XS, *piece), jnp.bfloat16),
            pltpu.VMEM((XS, *piece), jnp.bfloat16),
            pltpu.VMEM((2, XS, *piece), jnp.bfloat16),
            dma((3,)), dma((3,)), dma((11, XS)), dma((11, XS)), dma((11, XS)), dma((11, XS)), dma((11, 2, XS)),
            dma((3, XS)), dma((XS,)), dma((2, XS)), dma((2, XS)), dma((3,)),
        ],
        compiler_params=pltpu.CompilerParams(
            collective_id=1, has_side_effects=True, vmem_limit_bytes=32 * 2**20
        ),
        name="collect",
    )(dq_src, parts)


def by_head(rows):
    cut = rows.reshape(2, BLK, KV, GROUP, DIM).transpose(2, 0, 3, 1, 4)
    return cut.reshape(KV, 2, ROWS, DIM)


def lanes(rows):
    return rows.reshape(KV, GROUP, 2, BLK).transpose(0, 2, 1, 3).reshape(KV, 2, ROWS)


def on_device(query, key, value, output, grad_output, lse, doc_starts):
    window, z, x, core = place()
    delta = jnp.einsum("qhd,qhd->hq", grad_output, output, preferred_element_type=jnp.float32)
    rows = jnp.stack([lanes(lse * LOG2E), lanes(delta)], axis=2).reshape(KV, 4, ROWS)
    ld_src = jnp.concatenate([rows, jnp.zeros_like(rows)], axis=1)
    qd_src = jnp.stack([by_head(query), by_head(grad_output)], axis=1)
    kv_src = jnp.stack([key, value]).reshape(2, 2, BLK, KV, DIM).transpose(3, 0, 1, 2, 4)
    kv, qd, ld = spread(kv_src, qd_src, ld_src)
    info = jnp.stack([window, z, core, x]).astype(jnp.int32)
    dq, parts = grads(info, doc_starts, qd_src, ld_src, qd, ld, kv.reshape(2, KEY_ROWS, DIM))
    dq_back, dkv = collect(dq, parts.reshape(2, PAIRS, 2, BLK, DIM))
    grad_query = (
        dq_back.reshape(KV, 2, GROUP, BLK, DIM).transpose(1, 3, 0, 2, 4).reshape(2 * BLK, KV * GROUP, DIM)
    )
    back = dkv.transpose(1, 2, 3, 0, 4).reshape(2, 2 * BLK, KV, DIM)
    return grad_query, back[0], back[1]


def solution(mesh):
    tokens = P(("outer", "inner"), None, None)
    return jax.shard_map(
        on_device,
        mesh=mesh,
        in_specs=(tokens, tokens, tokens, tokens, tokens, P(None, ("outer", "inner")), P()),
        out_specs=(tokens, tokens, tokens),
        check_vma=False,
    )
```

time: 135 us -> 111 us (0.82)
  the two profiles are of different devices: /device:TPU:88 before, /device:TPU:16 now
where the time goes in v2:
time: 111 us
  Pallas kernels  95.7 us (86%)
  local copies, waits for them, and re-layouts  9.35 us (8%)
  other arithmetic  4.75 us (4%)
    pallas_call x1, Pallas kernels, spread(): pl.pallas_call(spread_kernel, out_shape=(jax.ShapeDtypeStruct((2, PAIRS,...  38.4 us
    pallas_call x1, Pallas kernels, collect(): pl.pallas_call(collect_kernel, out_shape=(jax.ShapeDtypeStruct(dq_src.sha...  32.1 us
    pallas_call x1, Pallas kernels, grads(): pl.pallas_call(grads_kernel, grid_spec=pltpu.PrefetchScalarGridSpec(num_s...  25.2 us
    unnamed x27, local copies, waits for them, and re-layouts  8.07 us

profile of v2, /device:TPU:16, one launch (start us, length us, event | category | flops | bytes accessed | tf_op | source)
XLA Modules:
  0.0 110.7 jit_solution(12132789667729593894)
XLA Ops:
  0.6 0.0 copy-start.9
  0.7 0.1 pad_add_fusion.info
  0.8 0.7 broadcast_multiply_fusion
  1.5 0.1 reshape.45
  1.6 0.1 stack_reshape.14
  1.7 1.9 %fusion = f32[24,128]{0,1:T(8,128)S(1)} fusion(bf16[128,24,128]{2,1,0:T(8,128)(2,1)} %param.10, bf16[128,24,128]{2,1,0:T(8,128)(2,1)} %param.11), kind=kLoop, calls=%fused_computation.2 | loop fusion | flops 1569792 | bytes 1585152
  3.6 0.1 copy.37
  3.6 0.1 reshape.46
  3.8 0.1 stack_reshape.15
  3.9 0.6 concatenate.4.ld_src.ld_own
  4.6 0.0 copy-done.8
  4.6 0.7 maximum_bitcast_fusion.kv_src
  5.4 0.2 copy.18
  5.5 0.1 copy.19
  5.6 0.9 copy-done.6
  6.5 0.2 copy.20
  6.7 0.1 copy.21
  6.7 1.3 %pad_maximum_fusion.qd_src.qd_own = bf16[4,2,2,384,128]{4,3,2,1,0:T(8,128)(2,1)} fusion(bf16[4,1,2,384,128]{4,3,2,1,0:T(8,128)(2,1)S(1)} %bitcast.41, bf16[4,1,2,384,128]{4,3,2,1,0:T(8,128)(2,1)S(1)} %bitcast.40), kind=kLoop, calls=%fused_computation | loop fusion | flops 786432 | bytes 3145728 | tf_op jit(solution)/shard_map/stack | solution.py:579
  8.0 38.4 %spread.1 = (bf16[2,46,2,64,128]{4,3,2,1,0:T(8,128)(2,1)}, bf16[3,2,2,384,128]{4,3,2,1,0:T(8,128)(2,1)}, f32[3,8,384]{2,1,0:T(8,128)}) custom-call(bf16[4,2,2,64,128]{4,3,2,1,0:T(8,128)(2,1)} %maximum_bitcast_fusion.kv_src, bf16[4,2,2,384,128]{4,3,2,1,0:T(8,128)(2,1)} %pad_maximum_fusion.qd_src.qd_own, f32[4,8,384]{2,1,0:T(8,128)} %concatenate.4.ld_src.ld_own), custom_call_target="tpu_custom_call" | custom-call | tf_op jit(solution)/shard_map/spread/pallas_call | solution.py:250
  46.4 0.0 copy-done
  46.4 0.0 copy-done.3
  46.4 0.0 copy-done.5
  46.5 0.0 copy-start.1
  46.5 1.8 %copy-done.1 = bf16[2,46,2,64,128]{4,3,2,1,0:T(8,128)(2,1)S(1)} copy-done((bf16[2,46,2,64,128]{4,3,2,1,0:T(8,128)(2,1)S(1)}, bf16[2,46,2,64,128]{4,3,2,1,0:T(8,128)(2,1)}, u32[]{:S(2)}) %copy-start.1) | copy-done | bytes 3014680
  48.3 1.3 %copy-done.2 = bf16[3,2,2,384,128]{4,3,2,1,0:T(8,128)(2,1)S(1)} copy-done((bf16[3,2,2,384,128]{4,3,2,1,0:T(8,128)(2,1)S(1)}, bf16[3,2,2,384,128]{4,3,2,1,0:T(8,128)(2,1)}, u32[]{:S(2)}) %copy-start.2) | copy-done | bytes 1179672
  49.6 0.8 copy-done.4
  50.4 25.2 %grads.1 = (bf16[4,2,384,128]{3,2,1,0:T(8,128)(2,1)S(1)}, bf16[2,5888,128]{2,1,0:T(8,128)(2,1)S(1)}) custom-call(s32[4]{0:T(128)S(1)} %pad_add_fusion.info, s32[24]{0:T(128)S(1)} %copy-done.5, bf16[4,2,2,384,128]{4,3,2,1,0:T(8,128)(2,1)S(1)} %copy-done, f32[4,8,384]{2,1,0:T(8,128)S(1)} %copy-done.3, bf16[3,2,2,384,128]{4,3,2,1,0:T(8,128)(2,1)S(1)} %copy-done.2, ...), custom_call_target="tpu_custom_call" | custom-call | tf_op jit(solution)/shard_map/grads/pallas_call | solution.py:332
  75.5 32.1 %collect.1 = (bf16[4,2,384,128]{3,2,1,0:T(8,128)(2,1)S(1)}, bf16[4,2,2,64,128]{4,3,2,1,0:T(8,128)(2,1)S(1)}) custom-call(bf16[4,2,384,128]{3,2,1,0:T(8,128)(2,1)S(1)} %get-tuple-element.13.dq_src, bf16[2,46,2,64,128]{4,3,2,1,0:T(8,128)(2,1)S(1)} %bitcast.34), custom_call_target="tpu_custom_call" | custom-call | tf_op jit(solution)/shard_map/collect/pallas_call | solution.py:540
  107.7 0.1 copy.27
  107.7 1.4 %copy.28 = bf16[128,24,128]{2,1,0:T(8,128)(2,1)} copy(bf16[128,24,128]{2,0,1:T(8,128)(2,1)S(1)} %bitcast.37) | data formatting | bytes 1572864
  109.1 0.8 copy.30
  109.9 0.8 copy.29
  (18 shorter events, 0.1 us)
Async XLA Ops:
  0.6 4.0 %copy-start.9 = (bf16[128,4,128]{2,1,0:T(4,128)(2,1)S(1)}, bf16[128,4,128]{2,1,0:T(4,128)(2,1)}, u32[]{:S(2)}) copy-start(bf16[128,4,128]{2,1,0:T(4,128)(2,1)} %param.9) | copy-start | bytes 393220
  0.6 3.9 %copy-start.8 = (bf16[128,4,128]{2,1,0:T(4,128)(2,1)S(1)}, bf16[128,4,128]{2,1,0:T(4,128)(2,1)}, u32[]{:S(2)}) copy-start(bf16[128,4,128]{2,1,0:T(4,128)(2,1)} %param.8) | copy-start | bytes 393220
  1.7 3.7 %copy-start.7 = (bf16[128,24,128]{2,1,0:T(8,128)(2,1)S(1)}, bf16[128,24,128]{2,1,0:T(8,128)(2,1)}, u32[]{:S(2)}) copy-start(bf16[128,24,128]{2,1,0:T(8,128)(2,1)} %param.7) | copy-start | bytes 2359300
  5.3 1.1 %copy-start.6 = (bf16[128,24,128]{2,1,0:T(8,128)(2,1)S(1)}, bf16[128,24,128]{2,1,0:T(8,128)(2,1)}, u32[]{:S(2)}) copy-start(bf16[128,24,128]{2,1,0:T(8,128)(2,1)} %param.11) | copy-start | bytes 2359300
  8.0 38.4 %copy-start = (bf16[4,2,2,384,128]{4,3,2,1,0:T(8,128)(2,1)S(1)}, bf16[4,2,2,384,128]{4,3,2,1,0:T(8,128)(2,1)}, u32[]{:S(2)}) copy-start(bf16[4,2,2,384,128]{4,3,2,1,0:T(8,128)(2,1)} %pad_maximum_fusion.qd_src.qd_own) | copy-start | bytes 4718596
  8.0 38.4 %copy-start.3 = (f32[4,8,384]{2,1,0:T(8,128)S(1)}, f32[4,8,384]{2,1,0:T(8,128)}, u32[]{:S(2)}) copy-start(f32[4,8,384]{2,1,0:T(8,128)} %concatenate.4.ld_src.ld_own) | copy-start | bytes 147460
  8.0 38.4 %copy-start.5 = (s32[24]{0:T(128)S(1)}, s32[24]{0:T(128)}, u32[]{:S(2)}) copy-start(s32[24]{0:T(128)} %starts.1) | copy-start | bytes 292
  46.5 1.9 %copy-start.1 = (bf16[2,46,2,64,128]{4,3,2,1,0:T(8,128)(2,1)S(1)}, bf16[2,46,2,64,128]{4,3,2,1,0:T(8,128)(2,1)}, u32[]{:S(2)}) copy-start(bf16[2,46,2,64,128]{4,3,2,1,0:T(8,128)(2,1)} %get-tuple-element.12) | copy-start | bytes 9043972
  48.3 1.3 %copy-start.2 = (bf16[3,2,2,384,128]{4,3,2,1,0:T(8,128)(2,1)S(1)}, bf16[3,2,2,384,128]{4,3,2,1,0:T(8,128)(2,1)}, u32[]{:S(2)}) copy-start(bf16[3,2,2,384,128]{4,3,2,1,0:T(8,128)(2,1)} %get-tuple-element.10.qd) | copy-start | bytes 3538948
  49.6 0.8 copy-start.4

commit v3 on v2

--- a/solution.py
+++ b/solution.py
@@ -265,7 +265,7 @@
     )(kv_src, qd_src, ld_src)
 
 
-def grads_kernel(info, starts, qd_own, ld_own, qd, ld, kv_hbm, dq, parts, kv, totals, dq_t, kv_sem):
+def grads_kernel(info, starts, qd_own, ld_own, qd, ld, kv_hbm, dq, parts, kv, totals, dq_t, held, kv_sem):
     step, half = pl.program_id(0), pl.program_id(1)
     window, z, core = info[0], info[1], info[2]
     src = (info[3] - step + XS) % XS
@@ -305,20 +305,32 @@
     delta = jnp.where(step == 0, ld_own[row_at, :], ld[row_at, :])
     dq_t[...] = jnp.zeros_like(dq_t)
 
-    @pl.loop(0, tiles)
-    def _(tile):
+    def scores(tile):
         row = pl.multiple_of(end - (tile + 1) * TILE, BLK)
         rows = pl.ds(row, TILE)
-        k, v = kv[0, rows, :], kv[1, rows, :]
-        s = lax.dot_general(k, q, (((1,), (1,)), ((), ())), preferred_element_type=jnp.float32)
-        dp = lax.dot_general(v, do, (((1,), (1,)), ((), ())), preferred_element_type=jnp.float32)
+        s = lax.dot_general(kv[0, rows, :], q, (((1,), (1,)), ((), ())), preferred_element_type=jnp.float32)
+        dp = lax.dot_general(kv[1, rows, :], do, (((1,), (1,)), ((), ())), preferred_element_type=jnp.float32)
         key_row = row + lax.broadcasted_iota(jnp.int32, (TILE, 1), 0)
         allowed = (key_row <= query_row) & (key_row >= query_from)
         p = jnp.where(allowed, jnp.exp2(s * (SCALE * LOG2E) - lse), 0.0)
-        ds = (p * (dp - delta)).astype(jnp.bfloat16)
-        totals[1, rows, :] += jnp.dot(p.astype(jnp.bfloat16), do, preferred_element_type=jnp.float32)
+        return p.astype(jnp.bfloat16), (p * (dp - delta)).astype(jnp.bfloat16)
+
+    def products(tile, p, ds):
+        rows = pl.ds(pl.multiple_of(end - (tile + 1) * TILE, BLK), TILE)
+        totals[1, rows, :] += jnp.dot(p, do, preferred_element_type=jnp.float32)
         totals[0, rows, :] += jnp.dot(ds, q, preferred_element_type=jnp.float32)
-        dq_t[...] += lax.dot_general(k, ds, (((0,), (0,)), ((), ())), preferred_element_type=jnp.float32)
+        dq_t[...] += lax.dot_general(kv[0, rows, :], ds, (((0,), (0,)), ((), ())), preferred_element_type=jnp.float32)
+
+    held[0], held[1] = scores(0)
+
+    @pl.loop(1, tiles)
+    def _(tile):
+        p, ds = held[0], held[1]
+        new_p, new_ds = scores(tile)
+        products(tile - 1, p, ds)
+        held[0], held[1] = new_p, new_ds
+
+    products(tiles - 1, held[0], held[1])
 
     dq[...] = (dq_t[...].T * SCALE).astype(jnp.bfloat16)
 
@@ -355,6 +367,7 @@
                 pltpu.VMEM((2, KEY_ROWS, DIM), jnp.bfloat16),
                 pltpu.VMEM((2, KEY_ROWS, DIM), jnp.float32),
                 pltpu.VMEM((DIM, ROWS), jnp.float32),
+                pltpu.VMEM((2, TILE, ROWS), jnp.bfloat16),
                 pltpu.SemaphoreType.DMA,
             ],
         ),

time: 111 us -> 110 us (level); the launches traced: 111 us -> 108 us
  Pallas kernels: 95.7 us -> 93.5 us
    pallas_call x1, Pallas kernels: 32.1 us -> 30.4 us  [collect(): pl.pallas_call(collect_kernel, out_shape=(jax.ShapeDtypeStruct(dq_src.sha...]
where the time goes in v3:
time: 110 us; the launch traced here: 108 us
  Pallas kernels  93.5 us (85%)
  local copies, waits for them, and re-layouts  9.35 us (8%)
  other arithmetic  4.75 us (4%)
    pallas_call x1, Pallas kernels, spread(): pl.pallas_call(spread_kernel, out_shape=(jax.ShapeDtypeStruct((2, PAIRS,...  38.4 us
    pallas_call x1, Pallas kernels, collect(): pl.pallas_call(collect_kernel, out_shape=(jax.ShapeDtypeStruct(dq_src.sha...  30.4 us
    pallas_call x1, Pallas kernels, grads(): pl.pallas_call(grads_kernel, grid_spec=pltpu.PrefetchScalarGridSpec(num_s...  24.6 us
    unnamed x27, local copies, waits for them, and re-layouts  8.07 us

profile of v3, /device:TPU:16, one launch (start us, length us, event | category | flops | bytes accessed | tf_op | source)
XLA Modules:
  0.0 108.4 jit_solution(8472594663196583269)
XLA Ops:
  0.6 0.0 copy-start.9
  0.7 0.1 pad_add_fusion.info
  0.8 0.7 broadcast_multiply_fusion
  1.5 0.1 reshape.45
  1.6 0.1 stack_reshape.14
  1.7 1.9 %fusion = f32[24,128]{0,1:T(8,128)S(1)} fusion(bf16[128,24,128]{2,1,0:T(8,128)(2,1)} %param.10, bf16[128,24,128]{2,1,0:T(8,128)(2,1)} %param.11), kind=kLoop, calls=%fused_computation.2 | loop fusion | flops 1569792 | bytes 1585152
  3.6 0.1 copy.37
  3.6 0.1 reshape.46
  3.8 0.1 stack_reshape.15
  3.9 0.6 concatenate.4.ld_src.ld_own
  4.6 0.0 copy-done.8
  4.6 0.7 maximum_bitcast_fusion.kv_src
  5.4 0.2 copy.18
  5.5 0.1 copy.19
  5.6 0.9 copy-done.6
  6.5 0.2 copy.20
  6.7 0.1 copy.21
  6.7 1.3 %pad_maximum_fusion.qd_src.qd_own = bf16[4,2,2,384,128]{4,3,2,1,0:T(8,128)(2,1)} fusion(bf16[4,1,2,384,128]{4,3,2,1,0:T(8,128)(2,1)S(1)} %bitcast.41, bf16[4,1,2,384,128]{4,3,2,1,0:T(8,128)(2,1)S(1)} %bitcast.40), kind=kLoop, calls=%fused_computation | loop fusion | flops 786432 | bytes 3145728 | tf_op jit(solution)/shard_map/stack | solution.py:592
  8.0 38.4 %spread.1 = (bf16[2,46,2,64,128]{4,3,2,1,0:T(8,128)(2,1)}, bf16[3,2,2,384,128]{4,3,2,1,0:T(8,128)(2,1)}, f32[3,8,384]{2,1,0:T(8,128)}) custom-call(bf16[4,2,2,64,128]{4,3,2,1,0:T(8,128)(2,1)} %maximum_bitcast_fusion.kv_src, bf16[4,2,2,384,128]{4,3,2,1,0:T(8,128)(2,1)} %pad_maximum_fusion.qd_src.qd_own, f32[4,8,384]{2,1,0:T(8,128)} %concatenate.4.ld_src.ld_own), custom_call_target="tpu_custom_call" | custom-call | tf_op jit(solution)/shard_map/spread/pallas_call | solution.py:250
  46.4 0.0 copy-done
  46.4 0.0 copy-done.3
  46.4 0.0 copy-done.5
  46.5 0.0 copy-start.1
  46.5 1.8 %copy-done.1 = bf16[2,46,2,64,128]{4,3,2,1,0:T(8,128)(2,1)S(1)} copy-done((bf16[2,46,2,64,128]{4,3,2,1,0:T(8,128)(2,1)S(1)}, bf16[2,46,2,64,128]{4,3,2,1,0:T(8,128)(2,1)}, u32[]{:S(2)}) %copy-start.1) | copy-done | bytes 3014680
  48.3 1.3 %copy-done.2 = bf16[3,2,2,384,128]{4,3,2,1,0:T(8,128)(2,1)S(1)} copy-done((bf16[3,2,2,384,128]{4,3,2,1,0:T(8,128)(2,1)S(1)}, bf16[3,2,2,384,128]{4,3,2,1,0:T(8,128)(2,1)}, u32[]{:S(2)}) %copy-start.2) | copy-done | bytes 1179672
  49.6 0.8 copy-done.4
  50.4 24.6 %grads.1 = (bf16[4,2,384,128]{3,2,1,0:T(8,128)(2,1)S(1)}, bf16[2,5888,128]{2,1,0:T(8,128)(2,1)S(1)}) custom-call(s32[4]{0:T(128)S(1)} %pad_add_fusion.info, s32[24]{0:T(128)S(1)} %copy-done.5, bf16[4,2,2,384,128]{4,3,2,1,0:T(8,128)(2,1)S(1)} %copy-done, f32[4,8,384]{2,1,0:T(8,128)S(1)} %copy-done.3, bf16[3,2,2,384,128]{4,3,2,1,0:T(8,128)(2,1)S(1)} %copy-done.2, ...), custom_call_target="tpu_custom_call" | custom-call | tf_op jit(solution)/shard_map/grads/pallas_call | solution.py:344
  75.0 30.4 %collect.1 = (bf16[4,2,384,128]{3,2,1,0:T(8,128)(2,1)S(1)}, bf16[4,2,2,64,128]{4,3,2,1,0:T(8,128)(2,1)S(1)}) custom-call(bf16[4,2,384,128]{3,2,1,0:T(8,128)(2,1)S(1)} %get-tuple-element.13.dq_src, bf16[2,46,2,64,128]{4,3,2,1,0:T(8,128)(2,1)S(1)} %bitcast.34), custom_call_target="tpu_custom_call" | custom-call | tf_op jit(solution)/shard_map/collect/pallas_call | solution.py:553
  105.4 0.1 copy.27
  105.5 1.4 %copy.28 = bf16[128,24,128]{2,1,0:T(8,128)(2,1)} copy(bf16[128,24,128]{2,0,1:T(8,128)(2,1)S(1)} %bitcast.37) | data formatting | bytes 1572864
  106.9 0.8 copy.30
  107.7 0.8 copy.29
  (18 shorter events, 0.1 us)
Async XLA Ops:
  0.6 4.0 %copy-start.9 = (bf16[128,4,128]{2,1,0:T(4,128)(2,1)S(1)}, bf16[128,4,128]{2,1,0:T(4,128)(2,1)}, u32[]{:S(2)}) copy-start(bf16[128,4,128]{2,1,0:T(4,128)(2,1)} %param.9) | copy-start | bytes 393220
  0.6 3.9 %copy-start.8 = (bf16[128,4,128]{2,1,0:T(4,128)(2,1)S(1)}, bf16[128,4,128]{2,1,0:T(4,128)(2,1)}, u32[]{:S(2)}) copy-start(bf16[128,4,128]{2,1,0:T(4,128)(2,1)} %param.8) | copy-start | bytes 393220
  1.7 3.7 %copy-start.7 = (bf16[128,24,128]{2,1,0:T(8,128)(2,1)S(1)}, bf16[128,24,128]{2,1,0:T(8,128)(2,1)}, u32[]{:S(2)}) copy-start(bf16[128,24,128]{2,1,0:T(8,128)(2,1)} %param.7) | copy-start | bytes 2359300
  5.3 1.1 %copy-start.6 = (bf16[128,24,128]{2,1,0:T(8,128)(2,1)S(1)}, bf16[128,24,128]{2,1,0:T(8,128)(2,1)}, u32[]{:S(2)}) copy-start(bf16[128,24,128]{2,1,0:T(8,128)(2,1)} %param.11) | copy-start | bytes 2359300
  8.0 38.4 %copy-start = (bf16[4,2,2,384,128]{4,3,2,1,0:T(8,128)(2,1)S(1)}, bf16[4,2,2,384,128]{4,3,2,1,0:T(8,128)(2,1)}, u32[]{:S(2)}) copy-start(bf16[4,2,2,384,128]{4,3,2,1,0:T(8,128)(2,1)} %pad_maximum_fusion.qd_src.qd_own) | copy-start | bytes 4718596
  8.0 38.4 %copy-start.3 = (f32[4,8,384]{2,1,0:T(8,128)S(1)}, f32[4,8,384]{2,1,0:T(8,128)}, u32[]{:S(2)}) copy-start(f32[4,8,384]{2,1,0:T(8,128)} %concatenate.4.ld_src.ld_own) | copy-start | bytes 147460
  8.0 38.4 %copy-start.5 = (s32[24]{0:T(128)S(1)}, s32[24]{0:T(128)}, u32[]{:S(2)}) copy-start(s32[24]{0:T(128)} %starts.1) | copy-start | bytes 292
  46.5 1.9 %copy-start.1 = (bf16[2,46,2,64,128]{4,3,2,1,0:T(8,128)(2,1)S(1)}, bf16[2,46,2,64,128]{4,3,2,1,0:T(8,128)(2,1)}, u32[]{:S(2)}) copy-start(bf16[2,46,2,64,128]{4,3,2,1,0:T(8,128)(2,1)} %get-tuple-element.12) | copy-start | bytes 9043972
  48.3 1.3 %copy-start.2 = (bf16[3,2,2,384,128]{4,3,2,1,0:T(8,128)(2,1)S(1)}, bf16[3,2,2,384,128]{4,3,2,1,0:T(8,128)(2,1)}, u32[]{:S(2)}) copy-start(bf16[3,2,2,384,128]{4,3,2,1,0:T(8,128)(2,1)} %get-tuple-element.10.qd) | copy-start | bytes 3538948
  49.6 0.8 copy-start.4

commit v4 on v3

--- a/solution.py
+++ b/solution.py
@@ -14,12 +14,12 @@
 WINDOWS = 8
 WIN_BLOCKS = 64
 WIN_ROWS = WIN_BLOCKS * BLK
-PAD_PAIRS, PRIOR_PAIRS = 2, 12
+PAD_PAIRS, PRIOR_PAIRS = 4, 12
 BASE_PAIRS = PAD_PAIRS + PRIOR_PAIRS
 PAIRS = BASE_PAIRS + WIN_BLOCKS // 2
 KEY_ROWS = PAIRS * 2 * BLK
 BASE_ROW = BASE_PAIRS * 2 * BLK
-TILE = 256
+TILE = 512
 SCALE = 1.0 / math.sqrt(DIM)
 LOG2E = math.log2(math.e)
 

time: 110 us -> 108 us (0.982)
  Pallas kernels: 93.5 us -> 92 us
    pallas_call x1, Pallas kernels: 24.6 us -> 23.2 us  [grads(): pl.pallas_call(grads_kernel, grid_spec=pltpu.PrefetchScalarGridSpec(num_s...]
where the time goes in v4:
time: 108 us; the launch traced here: 107 us
  Pallas kernels  92 us (85%)
  local copies, waits for them, and re-layouts  9.39 us (9%)
  other arithmetic  4.75 us (4%)
    pallas_call x1, Pallas kernels, spread(): pl.pallas_call(spread_kernel, out_shape=(jax.ShapeDtypeStruct((2, PAIRS,...  38.4 us
    pallas_call x1, Pallas kernels, collect(): pl.pallas_call(collect_kernel, out_shape=(jax.ShapeDtypeStruct(dq_src.sha...  30.4 us
    pallas_call x1, Pallas kernels, grads(): pl.pallas_call(grads_kernel, grid_spec=pltpu.PrefetchScalarGridSpec(num_s...  23.2 us
    unnamed x27, local copies, waits for them, and re-layouts  8.11 us

profile of v4, /device:TPU:16, one launch (start us, length us, event | category | flops | bytes accessed | tf_op | source)
XLA Modules:
  0.0 107.0 jit_solution(9142941893403919716)
XLA Ops:
  0.6 0.0 copy-start.9
  0.7 0.1 pad_add_fusion.info
  0.8 0.7 broadcast_multiply_fusion
  1.5 0.1 reshape.45
  1.6 0.1 stack_reshape.14
  1.7 1.9 %fusion = f32[24,128]{0,1:T(8,128)S(1)} fusion(bf16[128,24,128]{2,1,0:T(8,128)(2,1)} %param.10, bf16[128,24,128]{2,1,0:T(8,128)(2,1)} %param.11), kind=kLoop, calls=%fused_computation.2 | loop fusion | flops 1569792 | bytes 1585152
  3.6 0.1 copy.37
  3.6 0.1 reshape.46
  3.8 0.1 stack_reshape.15
  3.9 0.6 concatenate.4.ld_src.ld_own
  4.6 0.0 copy-done.8
  4.6 0.7 maximum_bitcast_fusion.kv_src
  5.4 0.2 copy.18
  5.5 0.1 copy.19
  5.6 0.9 copy-done.6
  6.5 0.2 copy.20
  6.7 0.1 copy.21
  6.7 1.3 %pad_maximum_fusion.qd_src.qd_own = bf16[4,2,2,384,128]{4,3,2,1,0:T(8,128)(2,1)} fusion(bf16[4,1,2,384,128]{4,3,2,1,0:T(8,128)(2,1)S(1)} %bitcast.41, bf16[4,1,2,384,128]{4,3,2,1,0:T(8,128)(2,1)S(1)} %bitcast.40), kind=kLoop, calls=%fused_computation | loop fusion | flops 786432 | bytes 3145728 | tf_op jit(solution)/shard_map/stack | solution.py:592
  8.0 38.4 %spread.1 = (bf16[2,48,2,64,128]{4,3,2,1,0:T(8,128)(2,1)}, bf16[3,2,2,384,128]{4,3,2,1,0:T(8,128)(2,1)}, f32[3,8,384]{2,1,0:T(8,128)}) custom-call(bf16[4,2,2,64,128]{4,3,2,1,0:T(8,128)(2,1)} %maximum_bitcast_fusion.kv_src, bf16[4,2,2,384,128]{4,3,2,1,0:T(8,128)(2,1)} %pad_maximum_fusion.qd_src.qd_own, f32[4,8,384]{2,1,0:T(8,128)} %concatenate.4.ld_src.ld_own), custom_call_target="tpu_custom_call" | custom-call | tf_op jit(solution)/shard_map/spread/pallas_call | solution.py:250
  46.4 0.0 copy-done
  46.4 0.0 copy-done.3
  46.4 0.0 copy-done.5
  46.5 0.0 copy-start.1
  46.5 1.9 %copy-done.1 = bf16[2,48,2,64,128]{4,3,2,1,0:T(8,128)(2,1)S(1)} copy-done((bf16[2,48,2,64,128]{4,3,2,1,0:T(8,128)(2,1)S(1)}, bf16[2,48,2,64,128]{4,3,2,1,0:T(8,128)(2,1)}, u32[]{:S(2)}) %copy-start.1) | copy-done | bytes 3145752
  48.3 1.3 %copy-done.2 = bf16[3,2,2,384,128]{4,3,2,1,0:T(8,128)(2,1)S(1)} copy-done((bf16[3,2,2,384,128]{4,3,2,1,0:T(8,128)(2,1)S(1)}, bf16[3,2,2,384,128]{4,3,2,1,0:T(8,128)(2,1)}, u32[]{:S(2)}) %copy-start.2) | copy-done | bytes 1179672
  49.6 0.8 copy-done.4
  50.4 23.2 %grads.1 = (bf16[4,2,384,128]{3,2,1,0:T(8,128)(2,1)S(1)}, bf16[2,6144,128]{2,1,0:T(8,128)(2,1)S(1)}) custom-call(s32[4]{0:T(128)S(1)} %pad_add_fusion.info, s32[24]{0:T(128)S(1)} %copy-done.5, bf16[4,2,2,384,128]{4,3,2,1,0:T(8,128)(2,1)S(1)} %copy-done, f32[4,8,384]{2,1,0:T(8,128)S(1)} %copy-done.3, bf16[3,2,2,384,128]{4,3,2,1,0:T(8,128)(2,1)S(1)} %copy-done.2, ...), custom_call_target="tpu_custom_call" | custom-call | tf_op jit(solution)/shard_map/grads/pallas_call | solution.py:344
  73.6 30.4 %collect.1 = (bf16[4,2,384,128]{3,2,1,0:T(8,128)(2,1)S(1)}, bf16[4,2,2,64,128]{4,3,2,1,0:T(8,128)(2,1)S(1)}) custom-call(bf16[4,2,384,128]{3,2,1,0:T(8,128)(2,1)S(1)} %get-tuple-element.13.dq_src, bf16[2,48,2,64,128]{4,3,2,1,0:T(8,128)(2,1)S(1)} %bitcast.34), custom_call_target="tpu_custom_call" | custom-call | tf_op jit(solution)/shard_map/collect/pallas_call | solution.py:553
  104.0 0.1 copy.27
  104.1 1.4 %copy.28 = bf16[128,24,128]{2,1,0:T(8,128)(2,1)} copy(bf16[128,24,128]{2,0,1:T(8,128)(2,1)S(1)} %bitcast.37) | data formatting | bytes 1572864
  105.5 0.8 copy.30
  106.3 0.8 copy.29
  (18 shorter events, 0.1 us)
Async XLA Ops:
  0.6 4.0 %copy-start.9 = (bf16[128,4,128]{2,1,0:T(4,128)(2,1)S(1)}, bf16[128,4,128]{2,1,0:T(4,128)(2,1)}, u32[]{:S(2)}) copy-start(bf16[128,4,128]{2,1,0:T(4,128)(2,1)} %param.9) | copy-start | bytes 393220
  0.6 3.9 %copy-start.8 = (bf16[128,4,128]{2,1,0:T(4,128)(2,1)S(1)}, bf16[128,4,128]{2,1,0:T(4,128)(2,1)}, u32[]{:S(2)}) copy-start(bf16[128,4,128]{2,1,0:T(4,128)(2,1)} %param.8) | copy-start | bytes 393220
  1.7 3.7 %copy-start.7 = (bf16[128,24,128]{2,1,0:T(8,128)(2,1)S(1)}, bf16[128,24,128]{2,1,0:T(8,128)(2,1)}, u32[]{:S(2)}) copy-start(bf16[128,24,128]{2,1,0:T(8,128)(2,1)} %param.7) | copy-start | bytes 2359300
  5.3 1.1 %copy-start.6 = (bf16[128,24,128]{2,1,0:T(8,128)(2,1)S(1)}, bf16[128,24,128]{2,1,0:T(8,128)(2,1)}, u32[]{:S(2)}) copy-start(bf16[128,24,128]{2,1,0:T(8,128)(2,1)} %param.11) | copy-start | bytes 2359300
  8.0 38.4 %copy-start = (bf16[4,2,2,384,128]{4,3,2,1,0:T(8,128)(2,1)S(1)}, bf16[4,2,2,384,128]{4,3,2,1,0:T(8,128)(2,1)}, u32[]{:S(2)}) copy-start(bf16[4,2,2,384,128]{4,3,2,1,0:T(8,128)(2,1)} %pad_maximum_fusion.qd_src.qd_own) | copy-start | bytes 4718596
  8.0 38.4 %copy-start.3 = (f32[4,8,384]{2,1,0:T(8,128)S(1)}, f32[4,8,384]{2,1,0:T(8,128)}, u32[]{:S(2)}) copy-start(f32[4,8,384]{2,1,0:T(8,128)} %concatenate.4.ld_src.ld_own) | copy-start | bytes 147460
  8.0 38.4 %copy-start.5 = (s32[24]{0:T(128)S(1)}, s32[24]{0:T(128)}, u32[]{:S(2)}) copy-start(s32[24]{0:T(128)} %starts.1) | copy-start | bytes 292
  46.5 1.9 %copy-start.1 = (bf16[2,48,2,64,128]{4,3,2,1,0:T(8,128)(2,1)S(1)}, bf16[2,48,2,64,128]{4,3,2,1,0:T(8,128)(2,1)}, u32[]{:S(2)}) copy-start(bf16[2,48,2,64,128]{4,3,2,1,0:T(8,128)(2,1)} %get-tuple-element.12) | copy-start | bytes 9437188
  48.3 1.3 %copy-start.2 = (bf16[3,2,2,384,128]{4,3,2,1,0:T(8,128)(2,1)S(1)}, bf16[3,2,2,384,128]{4,3,2,1,0:T(8,128)(2,1)}, u32[]{:S(2)}) copy-start(bf16[3,2,2,384,128]{4,3,2,1,0:T(8,128)(2,1)} %get-tuple-element.10.qd) | copy-start | bytes 3538948
  49.6 0.8 copy-start.4

commit v5 on v3

--- a/solution.py
+++ b/solution.py
@@ -265,12 +265,15 @@
     )(kv_src, qd_src, ld_src)
 
 
-def grads_kernel(info, starts, qd_own, ld_own, qd, ld, kv_hbm, dq, parts, kv, totals, dq_t, held, kv_sem):
-    step, half = pl.program_id(0), pl.program_id(1)
-    window, z, core = info[0], info[1], info[2]
-    src = (info[3] - step + XS) % XS
-
-    @pl.when((step == 0) & (half == 0))
+def grads_kernel(
+    info, starts, qd_own, ld_own, qd_a, ld_a, qd_b, ld_b, kv_hbm, dq, parts,
+    kv, totals, dq_t, held, q, do, kv_sem,
+):
+    pair, half = pl.program_id(0), pl.program_id(1)
+    window, z, core, x = info[0], info[1], info[2], info[3]
+    slot_a, slot_b = (x - 2 * pair) & 3, (x - 2 * pair - 1) & 3
+
+    @pl.when((pair == 0) & (half == 0))
     def _():
         load = pltpu.make_async_copy(kv_hbm, kv, kv_sem)
         load.start()
@@ -284,32 +287,40 @@
         pl.when((z >= 2) | (window == 0))(lambda: clear(2 * PAD_PAIRS, 2 * PRIOR_PAIRS))
         pl.when(z == 0)(lambda: clear(2 * BASE_PAIRS + 8, 8))
 
-    low = 8 * z + 2 * src + core
-    block = jnp.where(half == 0, low, WIN_BLOCKS - 1 - low)
+    low = 8 * z + 4 * pair + core
+    block_a = jnp.where(half == 0, low, WIN_BLOCKS - 1 - low)
+    block_b = jnp.where(half == 0, low + 2, WIN_BLOCKS - 3 - low)
     shift = BASE_ROW - window * WIN_ROWS
-    first = BASE_ROW + block * BLK
-    query_row = first + (lax.broadcasted_iota(jnp.int32, (1, ROWS), 1) & (BLK - 1))
-    query_from = jnp.zeros((1, ROWS), jnp.int32)
+    first = BASE_ROW + jnp.minimum(block_a, block_b) * BLK
+    lane = lax.broadcasted_iota(jnp.int32, (1, 2 * ROWS), 1)
+    query_row = BASE_ROW + jnp.where(lane < ROWS, block_a, block_b) * BLK + (lane & (BLK - 1))
+    query_from = jnp.zeros((1, 2 * ROWS), jnp.int32)
     begin = 0
     for entry in range(24):
         at = starts[entry] + shift
         query_from = jnp.where(query_row >= at, at, query_from)
         begin = jnp.where(first >= at, at, begin)
-    end = first + BLK
+    end = first + 3 * BLK
     tiles = (end - begin + TILE - 1) // TILE
-    q = jnp.where(step == 0, qd_own[0], qd[0])
-    do = jnp.where(step == 0, qd_own[1], qd[1])
-    row_at = pl.ds(2 * half, 1)
-    lse = jnp.where(step == 0, ld_own[row_at, :], ld[row_at, :])
-    row_at = pl.ds(2 * half + 1, 1)
-    delta = jnp.where(step == 0, ld_own[row_at, :], ld[row_at, :])
+    for at, slot, came in ((0, slot_a, qd_a), (ROWS, slot_b, qd_b)):
+        q[pl.ds(at, ROWS), :] = jnp.where(slot == 0, qd_own[0], came[0])
+        do[pl.ds(at, ROWS), :] = jnp.where(slot == 0, qd_own[1], came[1])
+
+    def lanes_of(row):
+        at = pl.ds(2 * half + row, 1)
+        return jnp.concatenate(
+            [jnp.where(slot == 0, ld_own[at, :], came[at, :]) for slot, came in ((slot_a, ld_a), (slot_b, ld_b))],
+            axis=1,
+        )
+
+    lse, delta = lanes_of(0), lanes_of(1)
     dq_t[...] = jnp.zeros_like(dq_t)
 
     def scores(tile):
         row = pl.multiple_of(end - (tile + 1) * TILE, BLK)
         rows = pl.ds(row, TILE)
-        s = lax.dot_general(kv[0, rows, :], q, (((1,), (1,)), ((), ())), preferred_element_type=jnp.float32)
-        dp = lax.dot_general(kv[1, rows, :], do, (((1,), (1,)), ((), ())), preferred_element_type=jnp.float32)
+        s = lax.dot_general(kv[0, rows, :], q[...], (((1,), (1,)), ((), ())), preferred_element_type=jnp.float32)
+        dp = lax.dot_general(kv[1, rows, :], do[...], (((1,), (1,)), ((), ())), preferred_element_type=jnp.float32)
         key_row = row + lax.broadcasted_iota(jnp.int32, (TILE, 1), 0)
         allowed = (key_row <= query_row) & (key_row >= query_from)
         p = jnp.where(allowed, jnp.exp2(s * (SCALE * LOG2E) - lse), 0.0)
@@ -317,8 +328,8 @@
 
     def products(tile, p, ds):
         rows = pl.ds(pl.multiple_of(end - (tile + 1) * TILE, BLK), TILE)
-        totals[1, rows, :] += jnp.dot(p, do, preferred_element_type=jnp.float32)
-        totals[0, rows, :] += jnp.dot(ds, q, preferred_element_type=jnp.float32)
+        totals[1, rows, :] += jnp.dot(p, do[...], preferred_element_type=jnp.float32)
+        totals[0, rows, :] += jnp.dot(ds, q[...], preferred_element_type=jnp.float32)
         dq_t[...] += lax.dot_general(kv[0, rows, :], ds, (((0,), (0,)), ((), ())), preferred_element_type=jnp.float32)
 
     held[0], held[1] = scores(0)
@@ -332,12 +343,18 @@
 
     products(tiles - 1, held[0], held[1])
 
-    dq[...] = (dq_t[...].T * SCALE).astype(jnp.bfloat16)
-
-    @pl.when((step == XS - 1) & (half == 1))
+    rows_out = (dq_t[...].T * SCALE).astype(jnp.bfloat16)
+    dq[slot_a, half] = rows_out[:ROWS]
+    dq[slot_b, half] = rows_out[ROWS:]
+
+    @pl.when((pair == 1) & (half == 1))
     def _():
         parts[0] = (totals[0] * SCALE).astype(jnp.bfloat16)
         parts[1] = totals[1].astype(jnp.bfloat16)
+
+
+def slot_at(info, pair, second):
+    return jnp.maximum(((info[3] - 2 * pair - second) & 3) - 1, 0)
 
 
 def grads(info, starts, qd_own, ld_own, qd, ld, kv):
@@ -345,29 +362,37 @@
         grads_kernel,
         grid_spec=pltpu.PrefetchScalarGridSpec(
             num_scalar_prefetch=2,
-            grid=(XS, 2),
+            grid=(2, 2),
             in_specs=[
-                pl.BlockSpec(
-                    (None, 2, None, ROWS, DIM),
-                    lambda s, h, info, _: (info[3], 0, jnp.where(s == 0, h, 1), 0, 0),
+                pl.BlockSpec((None, 2, None, ROWS, DIM), lambda s, h, info, _: (info[3], 0, h, 0, 0)),
+                pl.BlockSpec((None, 8, ROWS), lambda s, h, info, _: (info[3], 0, 0)),
+                *(
+                    spec
+                    for second in (0, 1)
+                    for spec in (
+                        pl.BlockSpec(
+                            (None, 2, None, ROWS, DIM),
+                            lambda s, h, info, _, second=second: (slot_at(info, s, second), 0, h, 0, 0),
+                        ),
+                        pl.BlockSpec(
+                            (None, 8, ROWS),
+                            lambda s, h, info, _, second=second: (slot_at(info, s, second), 0, 0),
+                        ),
+                    )
                 ),
-                pl.BlockSpec((None, 8, ROWS), lambda s, h, info, _: (info[3], 0, 0)),
-                pl.BlockSpec(
-                    (None, 2, None, ROWS, DIM),
-                    lambda s, h, *_: (jnp.maximum(s - 1, 0), 0, jnp.where(s == 0, 0, h), 0, 0),
-                ),
-                pl.BlockSpec((None, 8, ROWS), lambda s, h, *_: (jnp.maximum(s - 1, 0), 0, 0)),
                 pl.BlockSpec(memory_space=pl.ANY),
             ],
             out_specs=[
-                pl.BlockSpec((None, None, ROWS, DIM), lambda s, h, *_: (s, h, 0, 0)),
+                pl.BlockSpec((XS, 2, ROWS, DIM), lambda s, h, *_: (0, 0, 0, 0)),
                 pl.BlockSpec((2, KEY_ROWS, DIM), lambda s, h, *_: (0, 0, 0)),
             ],
             scratch_shapes=[
                 pltpu.VMEM((2, KEY_ROWS, DIM), jnp.bfloat16),
                 pltpu.VMEM((2, KEY_ROWS, DIM), jnp.float32),
-                pltpu.VMEM((DIM, ROWS), jnp.float32),
-                pltpu.VMEM((2, TILE, ROWS), jnp.bfloat16),
+                pltpu.VMEM((DIM, 2 * ROWS), jnp.float32),
+                pltpu.VMEM((2, TILE, 2 * ROWS), jnp.bfloat16),
+                pltpu.VMEM((2 * ROWS, DIM), jnp.bfloat16),
+                pltpu.VMEM((2 * ROWS, DIM), jnp.bfloat16),
                 pltpu.SemaphoreType.DMA,
             ],
         ),
@@ -379,7 +404,7 @@
             dimension_semantics=("arbitrary", "arbitrary"), vmem_limit_bytes=40 * 2**20
         ),
         name="grads",
-    )(info, starts, qd_own, ld_own, qd, ld, kv)
+    )(info, starts, qd_own, ld_own, qd, ld, qd, ld, kv)
 
 
 def collect_kernel(

time: 110 us -> 106 us (0.964)
  Pallas kernels: 93.5 us -> 89.5 us
    pallas_call x1, Pallas kernels: 24.6 us -> 20.7 us  [grads(): pl.pallas_call(grads_kernel, grid_spec=pltpu.PrefetchScalarGridSpec(num_s...]
where the time goes in v5:
time: 106 us; the launch traced here: 104 us
  Pallas kernels  89.5 us (84%)
  local copies, waits for them, and re-layouts  9.35 us (9%)
  other arithmetic  4.75 us (4%)
    pallas_call x1, Pallas kernels, spread(): pl.pallas_call(spread_kernel, out_shape=(jax.ShapeDtypeStruct((2, PAIRS,...  38.4 us
    pallas_call x1, Pallas kernels, collect(): pl.pallas_call(collect_kernel, out_shape=(jax.ShapeDtypeStruct(dq_src.sha...  30.4 us
    pallas_call x1, Pallas kernels, grads(): pl.pallas_call(grads_kernel, grid_spec=pltpu.PrefetchScalarGridSpec(num_s...  20.7 us
    unnamed x27, local copies, waits for them, and re-layouts  8.07 us

profile of v5, /device:TPU:16, one launch (start us, length us, event | category | flops | bytes accessed | tf_op | source)
XLA Modules:
  0.0 104.5 jit_solution(3367920394886352506)
XLA Ops:
  0.6 0.0 copy-start.9
  0.6 0.0 copy-start.8
  0.7 0.1 pad_add_fusion.info
  0.8 0.7 broadcast_multiply_fusion
  1.5 0.1 reshape.45
  1.6 0.1 stack_reshape.14
  1.7 1.9 %fusion = f32[24,128]{0,1:T(8,128)S(1)} fusion(bf16[128,24,128]{2,1,0:T(8,128)(2,1)} %param.10, bf16[128,24,128]{2,1,0:T(8,128)(2,1)} %param.11), kind=kLoop, calls=%fused_computation.2 | loop fusion | flops 1569792 | bytes 1585152
  3.6 0.1 copy.37
  3.6 0.1 reshape.46
  3.8 0.1 stack_reshape.15
  3.9 0.6 concatenate.4.ld_src.ld_own
  4.6 0.0 copy-done.8
  4.6 0.0 copy-done.9
  4.6 0.7 maximum_bitcast_fusion.kv_src
  5.3 0.0 copy-done.7
  5.4 0.2 copy.18
  5.5 0.1 copy.19
  5.6 0.9 copy-done.6
  6.5 0.2 copy.20
  6.7 0.1 copy.21
  6.7 1.3 %pad_maximum_fusion.qd_src.qd_own = bf16[4,2,2,384,128]{4,3,2,1,0:T(8,128)(2,1)} fusion(bf16[4,1,2,384,128]{4,3,2,1,0:T(8,128)(2,1)S(1)} %bitcast.41, bf16[4,1,2,384,128]{4,3,2,1,0:T(8,128)(2,1)S(1)} %bitcast.40), kind=kLoop, calls=%fused_computation | loop fusion | flops 786432 | bytes 3145728 | tf_op jit(solution)/shard_map/stack | solution.py:617
  8.0 38.4 %spread.1 = (bf16[2,46,2,64,128]{4,3,2,1,0:T(8,128)(2,1)}, bf16[3,2,2,384,128]{4,3,2,1,0:T(8,128)(2,1)}, f32[3,8,384]{2,1,0:T(8,128)}) custom-call(bf16[4,2,2,64,128]{4,3,2,1,0:T(8,128)(2,1)} %maximum_bitcast_fusion.kv_src, bf16[4,2,2,384,128]{4,3,2,1,0:T(8,128)(2,1)} %pad_maximum_fusion.qd_src.qd_own, f32[4,8,384]{2,1,0:T(8,128)} %concatenate.4.ld_src.ld_own), custom_call_target="tpu_custom_call" | custom-call | tf_op jit(solution)/shard_map/spread/pallas_call | solution.py:250
  46.4 0.0 copy-done
  46.5 1.3 %copy-done.1 = bf16[3,2,2,384,128]{4,3,2,1,0:T(8,128)(2,1)S(1)} copy-done((bf16[3,2,2,384,128]{4,3,2,1,0:T(8,128)(2,1)S(1)}, bf16[3,2,2,384,128]{4,3,2,1,0:T(8,128)(2,1)}, u32[]{:S(2)}) %copy-start.1) | copy-done | bytes 1179672
  47.7 1.9 %copy-done.2 = bf16[2,46,2,64,128]{4,3,2,1,0:T(8,128)(2,1)S(1)} copy-done((bf16[2,46,2,64,128]{4,3,2,1,0:T(8,128)(2,1)S(1)}, bf16[2,46,2,64,128]{4,3,2,1,0:T(8,128)(2,1)}, u32[]{:S(2)}) %copy-start.2) | copy-done | bytes 3014680
  49.6 0.8 copy-done.4
  50.4 20.7 %grads.1 = (bf16[4,2,384,128]{3,2,1,0:T(8,128)(2,1)S(1)}, bf16[2,5888,128]{2,1,0:T(8,128)(2,1)S(1)}) custom-call(s32[4]{0:T(128)S(1)} %pad_add_fusion.info, s32[24]{0:T(128)S(1)} %copy-done.5, bf16[4,2,2,384,128]{4,3,2,1,0:T(8,128)(2,1)S(1)} %copy-done, f32[4,8,384]{2,1,0:T(8,128)S(1)} %copy-done.3, bf16[3,2,2,384,128]{4,3,2,1,0:T(8,128)(2,1)S(1)} %copy-done.1, ...), custom_call_target="tpu_custom_call" | custom-call | tf_op jit(solution)/shard_map/grads/pallas_call | solution.py:361
  71.0 30.4 %collect.1 = (bf16[4,2,384,128]{3,2,1,0:T(8,128)(2,1)S(1)}, bf16[4,2,2,64,128]{4,3,2,1,0:T(8,128)(2,1)S(1)}) custom-call(bf16[4,2,384,128]{3,2,1,0:T(8,128)(2,1)S(1)} %get-tuple-element.13.dq_src, bf16[2,46,2,64,128]{4,3,2,1,0:T(8,128)(2,1)S(1)} %bitcast.34), custom_call_target="tpu_custom_call" | custom-call | tf_op jit(solution)/shard_map/collect/pallas_call | solution.py:578
  101.5 0.1 copy.27
  101.5 1.4 %copy.28 = bf16[128,24,128]{2,1,0:T(8,128)(2,1)} copy(bf16[128,24,128]{2,0,1:T(8,128)(2,1)S(1)} %bitcast.37) | data formatting | bytes 1572864
  102.9 0.8 copy.30
  103.7 0.8 copy.29
  (18 shorter events, 0.1 us)
Async XLA Ops:
  0.6 4.0 %copy-start.9 = (bf16[128,4,128]{2,1,0:T(4,128)(2,1)S(1)}, bf16[128,4,128]{2,1,0:T(4,128)(2,1)}, u32[]{:S(2)}) copy-start(bf16[128,4,128]{2,1,0:T(4,128)(2,1)} %param.9) | copy-start | bytes 393220
  0.6 3.9 %copy-start.8 = (bf16[128,4,128]{2,1,0:T(4,128)(2,1)S(1)}, bf16[128,4,128]{2,1,0:T(4,128)(2,1)}, u32[]{:S(2)}) copy-start(bf16[128,4,128]{2,1,0:T(4,128)(2,1)} %param.8) | copy-start | bytes 393220
  1.7 3.7 %copy-start.7 = (bf16[128,24,128]{2,1,0:T(8,128)(2,1)S(1)}, bf16[128,24,128]{2,1,0:T(8,128)(2,1)}, u32[]{:S(2)}) copy-start(bf16[128,24,128]{2,1,0:T(8,128)(2,1)} %param.7) | copy-start | bytes 2359300
  5.3 1.1 %copy-start.6 = (bf16[128,24,128]{2,1,0:T(8,128)(2,1)S(1)}, bf16[128,24,128]{2,1,0:T(8,128)(2,1)}, u32[]{:S(2)}) copy-start(bf16[128,24,128]{2,1,0:T(8,128)(2,1)} %param.11) | copy-start | bytes 2359300
  8.0 38.4 %copy-start = (bf16[4,2,2,384,128]{4,3,2,1,0:T(8,128)(2,1)S(1)}, bf16[4,2,2,384,128]{4,3,2,1,0:T(8,128)(2,1)}, u32[]{:S(2)}) copy-start(bf16[4,2,2,384,128]{4,3,2,1,0:T(8,128)(2,1)} %pad_maximum_fusion.qd_src.qd_own) | copy-start | bytes 4718596
  8.0 38.4 %copy-start.3 = (f32[4,8,384]{2,1,0:T(8,128)S(1)}, f32[4,8,384]{2,1,0:T(8,128)}, u32[]{:S(2)}) copy-start(f32[4,8,384]{2,1,0:T(8,128)} %concatenate.4.ld_src.ld_own) | copy-start | bytes 147460
  8.0 38.4 %copy-start.5 = (s32[24]{0:T(128)S(1)}, s32[24]{0:T(128)}, u32[]{:S(2)}) copy-start(s32[24]{0:T(128)} %starts.1) | copy-start | bytes 292
  46.5 1.3 %copy-start.1 = (bf16[3,2,2,384,128]{4,3,2,1,0:T(8,128)(2,1)S(1)}, bf16[3,2,2,384,128]{4,3,2,1,0:T(8,128)(2,1)}, u32[]{:S(2)}) copy-start(bf16[3,2,2,384,128]{4,3,2,1,0:T(8,128)(2,1)} %get-tuple-element.10.qd_a.qd_b) | copy-start | bytes 3538948
  47.7 1.9 %copy-start.2 = (bf16[2,46,2,64,128]{4,3,2,1,0:T(8,128)(2,1)S(1)}, bf16[2,46,2,64,128]{4,3,2,1,0:T(8,128)(2,1)}, u32[]{:S(2)}) copy-start(bf16[2,46,2,64,128]{4,3,2,1,0:T(8,128)(2,1)} %get-tuple-element.12) | copy-start | bytes 9043972
  49.6 0.8 copy-start.4

commit v6 on v5

--- a/solution.py
+++ b/solution.py
@@ -534,9 +534,8 @@
             else:
                 z_copy(gid, j, at, towards(gid)).wait_send()
 
-        @pl.loop(0, XS)
-        def _(j):
-            each((*order, *mine), begin, j)
+        for gid in (*order, *mine):
+            each([gid], lambda gid, _: pl.loop(0, XS)(lambda j: begin(gid, j)), None)
 
         dq_own.start()
         for step in (2, 1, 3):

time: 106 us -> 106 us (level)
    pallas_call x1, Pallas kernels: 30.4 us -> 32.8 us  [collect(): pl.pallas_call(collect_kernel, out_shape=(jax.ShapeDtypeStruct(dq_src.sha...]
    pallas_call x1, Pallas kernels: 20.7 us -> 19.2 us  [grads(): pl.pallas_call(grads_kernel, grid_spec=pltpu.PrefetchScalarGridSpec(num_s...]
where the time goes in v6:
time: 106 us; the launch traced here: 105 us
  Pallas kernels  90.5 us (85%)
  local copies, waits for them, and re-layouts  9.35 us (9%)
  other arithmetic  4.75 us (4%)
    pallas_call x1, Pallas kernels, spread(): pl.pallas_call(spread_kernel, out_shape=(jax.ShapeDtypeStruct((2, PAIRS,...  38.4 us
    pallas_call x1, Pallas kernels, collect(): pl.pallas_call(collect_kernel, out_shape=(jax.ShapeDtypeStruct(dq_src.sha...  32.8 us
    pallas_call x1, Pallas kernels, grads(): pl.pallas_call(grads_kernel, grid_spec=pltpu.PrefetchScalarGridSpec(num_s...  19.2 us
    unnamed x27, local copies, waits for them, and re-layouts  8.07 us

profile of v6, /device:TPU:16, one launch (start us, length us, event | category | flops | bytes accessed | tf_op | source)
XLA Modules:
  0.0 105.4 jit_solution(13883698381467723150)
XLA Ops:
  0.6 0.0 copy-start.9
  0.6 0.0 copy-start.8
  0.7 0.1 pad_add_fusion.info
  0.8 0.7 broadcast_multiply_fusion
  1.5 0.1 reshape.45
  1.6 0.1 stack_reshape.14
  1.7 1.9 %fusion = f32[24,128]{0,1:T(8,128)S(1)} fusion(bf16[128,24,128]{2,1,0:T(8,128)(2,1)} %param.10, bf16[128,24,128]{2,1,0:T(8,128)(2,1)} %param.11), kind=kLoop, calls=%fused_computation.2 | loop fusion | flops 1569792 | bytes 1585152
  3.6 0.1 copy.37
  3.6 0.1 reshape.46
  3.8 0.1 stack_reshape.15
  3.9 0.6 concatenate.4.ld_src.ld_own
  4.6 0.0 copy-done.8
  4.6 0.0 copy-done.9
  4.6 0.7 maximum_bitcast_fusion.kv_src
  5.3 0.0 copy-done.7
  5.4 0.2 copy.18
  5.5 0.1 copy.19
  5.6 0.9 copy-done.6
  6.5 0.2 copy.20
  6.7 0.1 copy.21
  6.7 1.3 %pad_maximum_fusion.qd_src.qd_own = bf16[4,2,2,384,128]{4,3,2,1,0:T(8,128)(2,1)} fusion(bf16[4,1,2,384,128]{4,3,2,1,0:T(8,128)(2,1)S(1)} %bitcast.41, bf16[4,1,2,384,128]{4,3,2,1,0:T(8,128)(2,1)S(1)} %bitcast.40), kind=kLoop, calls=%fused_computation | loop fusion | flops 786432 | bytes 3145728 | tf_op jit(solution)/shard_map/stack | solution.py:616
  8.0 38.4 %spread.1 = (bf16[2,46,2,64,128]{4,3,2,1,0:T(8,128)(2,1)}, bf16[3,2,2,384,128]{4,3,2,1,0:T(8,128)(2,1)}, f32[3,8,384]{2,1,0:T(8,128)}) custom-call(bf16[4,2,2,64,128]{4,3,2,1,0:T(8,128)(2,1)} %maximum_bitcast_fusion.kv_src, bf16[4,2,2,384,128]{4,3,2,1,0:T(8,128)(2,1)} %pad_maximum_fusion.qd_src.qd_own, f32[4,8,384]{2,1,0:T(8,128)} %concatenate.4.ld_src.ld_own), custom_call_target="tpu_custom_call" | custom-call | tf_op jit(solution)/shard_map/spread/pallas_call | solution.py:250
  46.4 0.0 copy-done
  46.5 1.3 %copy-done.1 = bf16[3,2,2,384,128]{4,3,2,1,0:T(8,128)(2,1)S(1)} copy-done((bf16[3,2,2,384,128]{4,3,2,1,0:T(8,128)(2,1)S(1)}, bf16[3,2,2,384,128]{4,3,2,1,0:T(8,128)(2,1)}, u32[]{:S(2)}) %copy-start.1) | copy-done | bytes 1179672
  47.7 1.9 %copy-done.2 = bf16[2,46,2,64,128]{4,3,2,1,0:T(8,128)(2,1)S(1)} copy-done((bf16[2,46,2,64,128]{4,3,2,1,0:T(8,128)(2,1)S(1)}, bf16[2,46,2,64,128]{4,3,2,1,0:T(8,128)(2,1)}, u32[]{:S(2)}) %copy-start.2) | copy-done | bytes 3014680
  49.6 0.8 copy-done.4
  50.4 19.2 %grads.1 = (bf16[4,2,384,128]{3,2,1,0:T(8,128)(2,1)S(1)}, bf16[2,5888,128]{2,1,0:T(8,128)(2,1)S(1)}) custom-call(s32[4]{0:T(128)S(1)} %pad_add_fusion.info, s32[24]{0:T(128)S(1)} %copy-done.5, bf16[4,2,2,384,128]{4,3,2,1,0:T(8,128)(2,1)S(1)} %copy-done, f32[4,8,384]{2,1,0:T(8,128)S(1)} %copy-done.3, bf16[3,2,2,384,128]{4,3,2,1,0:T(8,128)(2,1)S(1)} %copy-done.1, ...), custom_call_target="tpu_custom_call" | custom-call | tf_op jit(solution)/shard_map/grads/pallas_call | solution.py:361
  69.6 32.8 %collect.1 = (bf16[4,2,384,128]{3,2,1,0:T(8,128)(2,1)S(1)}, bf16[4,2,2,64,128]{4,3,2,1,0:T(8,128)(2,1)S(1)}) custom-call(bf16[4,2,384,128]{3,2,1,0:T(8,128)(2,1)S(1)} %get-tuple-element.13.dq_src, bf16[2,46,2,64,128]{4,3,2,1,0:T(8,128)(2,1)S(1)} %bitcast.34), custom_call_target="tpu_custom_call" | custom-call | tf_op jit(solution)/shard_map/collect/pallas_call | solution.py:577
  102.4 0.1 copy.27
  102.5 1.4 %copy.28 = bf16[128,24,128]{2,1,0:T(8,128)(2,1)} copy(bf16[128,24,128]{2,0,1:T(8,128)(2,1)S(1)} %bitcast.37) | data formatting | bytes 1572864
  103.9 0.8 copy.30
  104.7 0.8 copy.29
  (18 shorter events, 0.1 us)
Async XLA Ops:
  0.6 4.0 %copy-start.9 = (bf16[128,4,128]{2,1,0:T(4,128)(2,1)S(1)}, bf16[128,4,128]{2,1,0:T(4,128)(2,1)}, u32[]{:S(2)}) copy-start(bf16[128,4,128]{2,1,0:T(4,128)(2,1)} %param.9) | copy-start | bytes 393220
  0.6 3.9 %copy-start.8 = (bf16[128,4,128]{2,1,0:T(4,128)(2,1)S(1)}, bf16[128,4,128]{2,1,0:T(4,128)(2,1)}, u32[]{:S(2)}) copy-start(bf16[128,4,128]{2,1,0:T(4,128)(2,1)} %param.8) | copy-start | bytes 393220
  1.7 3.7 %copy-start.7 = (bf16[128,24,128]{2,1,0:T(8,128)(2,1)S(1)}, bf16[128,24,128]{2,1,0:T(8,128)(2,1)}, u32[]{:S(2)}) copy-start(bf16[128,24,128]{2,1,0:T(8,128)(2,1)} %param.7) | copy-start | bytes 2359300
  5.3 1.1 %copy-start.6 = (bf16[128,24,128]{2,1,0:T(8,128)(2,1)S(1)}, bf16[128,24,128]{2,1,0:T(8,128)(2,1)}, u32[]{:S(2)}) copy-start(bf16[128,24,128]{2,1,0:T(8,128)(2,1)} %param.11) | copy-start | bytes 2359300
  8.0 38.4 %copy-start = (bf16[4,2,2,384,128]{4,3,2,1,0:T(8,128)(2,1)S(1)}, bf16[4,2,2,384,128]{4,3,2,1,0:T(8,128)(2,1)}, u32[]{:S(2)}) copy-start(bf16[4,2,2,384,128]{4,3,2,1,0:T(8,128)(2,1)} %pad_maximum_fusion.qd_src.qd_own) | copy-start | bytes 4718596
  8.0 38.4 %copy-start.3 = (f32[4,8,384]{2,1,0:T(8,128)S(1)}, f32[4,8,384]{2,1,0:T(8,128)}, u32[]{:S(2)}) copy-start(f32[4,8,384]{2,1,0:T(8,128)} %concatenate.4.ld_src.ld_own) | copy-start | bytes 147460
  8.0 38.4 %copy-start.5 = (s32[24]{0:T(128)S(1)}, s32[24]{0:T(128)}, u32[]{:S(2)}) copy-start(s32[24]{0:T(128)} %starts.1) | copy-start | bytes 292
  46.5 1.3 %copy-start.1 = (bf16[3,2,2,384,128]{4,3,2,1,0:T(8,128)(2,1)S(1)}, bf16[3,2,2,384,128]{4,3,2,1,0:T(8,128)(2,1)}, u32[]{:S(2)}) copy-start(bf16[3,2,2,384,128]{4,3,2,1,0:T(8,128)(2,1)} %get-tuple-element.10.qd_a.qd_b) | copy-start | bytes 3538948
  47.7 1.9 %copy-start.2 = (bf16[2,46,2,64,128]{4,3,2,1,0:T(8,128)(2,1)S(1)}, bf16[2,46,2,64,128]{4,3,2,1,0:T(8,128)(2,1)}, u32[]{:S(2)}) copy-start(bf16[2,46,2,64,128]{4,3,2,1,0:T(8,128)(2,1)} %get-tuple-element.12) | copy-start | bytes 9043972
  49.6 0.8 copy-start.4
